TPU v7x, 256 devices: a whole 4x4x8 slice. The times are simulated.
256 devices in a mesh: member: 8 (over y, x_hi), domain: 32 (over z, x_lo, core).
Axes of the slice: x: 4 (x_hi: 2, x_lo: 2; x = x_hi * 2 + x_lo), y: 4, z: 8, core: 2. Of those that a mesh axis runs over, the one named last changes fastest.
Arguments:
- tracer: float32 [64, 3, 512, 1024], P('member', None, 'domain'), may hold values from -6 to 6
- east_speed: float32 [64, 512, 1024], P('member', 'domain'), may hold values from -0.35 to 0.35
- north_speed: float32 [64, 512, 1024], P('member', 'domain'), may hold values from -0.35 to 0.35
- diffusivity: float32 [64], replicated, may hold values from 0.02 to 0.07
- obs_cell: int32 [2, 64, 3], replicated, may hold values from 0 to 1023, as said below
- tile_offset: int32 [2, 64, 2], replicated, may hold values from 0 to 960, as said below
- obs_value: float32 [2, 64], replicated, may hold values from -6 to 6
- obs_error: float32 [2, 64], replicated, may hold values from 0.2 to 1
Outputs:
- analysis: float32 [64, 3, 512, 1024], P(None, None, 'domain', 'member')
Inputs may be any that keep to these rules, and one draw needn't show every extreme that they name: `obs_cell`: each row is (level, first index, second index) of a grid cell: level below 3, first index below 512, second below 1024. `tile_offset`: each observation's tile of 32 x 64 cells lies inside the grid and contains the observation's cell.
All inputs are finite; a program needn't handle non-finite values.
Results may differ from a plain program's by a relative error of at most 0.0001.
Values sent between devices are 32-bit elements; how exact they have to be, the bound alone decides.
No kernel may reach another device: no remote copies, remote signals or barrier semaphores. Data moves between devices by JAX's collectives and lax.ppermute only.
A program may use at most 128 MiB of HBM per device.

v0:
```python
import jax
import jax.numpy as jnp
from jax import lax
from jax.sharding import PartitionSpec as P

TILE_X = 32
TILE_Y = 64


def padded(array, sides, width):
    for axis, dim in sides:
        peers, length = (lax.axis_size(axis), array.shape[dim])
        up = [(i, (i + 1) % peers) for i in range(peers)]
        down = [(j, i) for i, j in up]
        last = lax.slice_in_dim(array, length - width, length, axis=dim)
        leading = lax.slice_in_dim(array, 0, width, axis=dim)
        before = lax.ppermute(last, axis, up)
        after = lax.ppermute(leading, axis, down)
        array = jnp.concatenate([before, array, after], axis=dim)
    return array


def concentration_change(halo_padded, depth_levels, diff_rates, wall_mask):
    tracer = halo_padded[:, :depth_levels]
    east_vel = halo_padded[:, depth_levels]
    north_vel = halo_padded[:, depth_levels + 1]
    rate_col = diff_rates[:, None, None, None]
    east_face = 0.5 * (east_vel[:, :-1, 1:-1] + east_vel[:, 1:, 1:-1])
    behind = tracer[:, :, :-1, 1:-1]
    ahead_cells = tracer[:, :, 1:, 1:-1]
    flux_east = (
        jnp.maximum(east_face, 0.0)[:, None] * behind
        + jnp.minimum(east_face, 0.0)[:, None] * ahead_cells
        - rate_col * (ahead_cells - behind)
    )
    north_face = 0.5 * (north_vel[:, 1:-1, :-1] + north_vel[:, 1:-1, 1:])
    lower_cells = tracer[:, :, 1:-1, :-1]
    upper_cells = tracer[:, :, 1:-1, 1:]
    flux_north = (
        jnp.maximum(north_face, 0.0)[:, None] * lower_cells
        + jnp.minimum(north_face, 0.0)[:, None] * upper_cells
        - rate_col * (upper_cells - lower_cells)
    ) * wall_mask
    centre = tracer[:, :, 1:-1, 1:-1]
    return (
        centre
        - (flux_east[:, :, 1:] - flux_east[:, :, :-1])
        - (flux_north[..., 1:] - flux_north[..., :-1])
    )


def closed_edge_flags(face_count, whole_grid_lines):
    face_ids = jnp.arange(face_count + 1)
    return jnp.where((face_ids == 0) | (face_ids == whole_grid_lines), 0.0, 1.0).astype(jnp.float32)


def taper(position, centre, first_cell, tile_span):
    inside = (position >= first_cell) & (position < first_cell + tile_span)
    return jnp.where(inside, 1.0 - jnp.abs(position - centre).astype(jnp.float32) / tile_span, 0.0)


def localize(level_ids, col_ids, row_ids, obs_level, obs_col, obs_row, start_col, start_row):
    vertical = jnp.where(level_ids == obs_level, 1.0, 0.5)
    across = taper(col_ids, obs_col, start_col, TILE_X)
    along = taper(row_ids, obs_row, start_row, TILE_Y)
    return vertical[:, None, None] * across[None, :, None] * along[None, None, :]


def innovation(priors, obs_index, obs_values, obs_errors):
    members = priors.shape[1]
    current = priors[obs_index]
    average = jnp.mean(current)
    spread = current - average
    variance = jnp.sum(spread * spread) / (members - 1)
    measurement_noise = obs_errors[obs_index]
    divisor_term = variance + measurement_noise
    reduction = 1.0 / (1.0 + jnp.sqrt(measurement_noise / divisor_term))
    correction = obs_values[obs_index] - average - reduction * spread
    factor = 1.0 / ((members - 1) * divisor_term)
    return (spread, correction, factor)


def update_priors(
    priors, spread, correction, factor, obs_cells, obs_level, obs_col, obs_row, start_col, start_row
):
    obs_cov = jnp.dot(priors, spread, precision=lax.Precision.HIGHEST)
    obs_weight = (
        jnp.where(obs_cells[:, 0] == obs_level, 1.0, 0.5)
        * taper(obs_cells[:, 1], obs_col, start_col, TILE_X)
        * taper(obs_cells[:, 2], obs_row, start_row, TILE_Y)
    )
    return priors + (obs_weight * obs_cov * factor)[:, None] * correction[None, :]


def block_priors(ensemble_fields, obs_cells, col_start, row_start):
    members, depth_levels, own_cols, own_rows = ensemble_fields.shape
    flat_block = ensemble_fields.reshape(members, depth_levels * own_cols * own_rows)
    inside = (
        (obs_cells[:, 1] >= col_start)
        & (obs_cells[:, 1] < col_start + own_cols)
        & (obs_cells[:, 2] >= row_start)
        & (obs_cells[:, 2] < row_start + own_rows)
    )
    flat_index = jnp.where(
        inside,
        obs_cells[:, 0] * (own_cols * own_rows)
        + (obs_cells[:, 1] - col_start) * own_rows
        + (obs_cells[:, 2] - row_start),
        0,
    )
    picked = jnp.where(inside[:, None], jnp.take(flat_block, flat_index, axis=1).T, 0.0)
    return lax.psum(picked, ("member", "domain"))


def filter_batch(
    ensemble_fields, priors, obs_cells, obs_tiles, obs_values, obs_errors, col_start, row_start
):
    members, depth_levels, own_cols, own_rows = ensemble_fields.shape
    level_ids = jnp.arange(depth_levels, dtype=jnp.int32)
    col_ids = col_start + jnp.arange(own_cols, dtype=jnp.int32)
    zero_index = jnp.zeros((), jnp.int32)

    def serial_step(obs_index, carried):
        ensemble_fields, priors = carried
        spread, correction, factor = innovation(priors, obs_index, obs_values, obs_errors)
        obs_level = obs_cells[obs_index, 0]
        obs_col = obs_cells[obs_index, 1]
        obs_row = obs_cells[obs_index, 2]
        start_col = obs_tiles[obs_index, 0]
        start_row = obs_tiles[obs_index, 1]
        touches = (
            (start_col < col_start + own_cols)
            & (start_col + TILE_X > col_start)
            & (start_row < row_start + own_rows)
            & (start_row + TILE_Y > row_start)
        )
        window_row = jnp.clip(start_row - row_start, 0, own_rows - TILE_Y)

        def apply_update(block):
            window = lax.dynamic_slice(
                block,
                (zero_index, zero_index, zero_index, window_row),
                (members, depth_levels, own_cols, TILE_Y),
            )
            row_ids = row_start + window_row + jnp.arange(TILE_Y, dtype=jnp.int32)
            weight = localize(
                level_ids, col_ids, row_ids, obs_level, obs_col, obs_row, start_col, start_row
            )
            covariance = jnp.einsum("mlxy,m->lxy", window, spread, precision=lax.Precision.HIGHEST)
            window = window + (weight * covariance * factor)[None] * correction[:, None, None, None]
            return lax.dynamic_update_slice(
                block, window, (zero_index, zero_index, zero_index, window_row)
            )

        def keep_block(block):
            return block

        ensemble_fields = lax.cond(touches, apply_update, keep_block, ensemble_fields)
        priors = update_priors(
            priors,
            spread,
            correction,
            factor,
            obs_cells,
            obs_level,
            obs_col,
            obs_row,
            start_col,
            start_row,
        )
        return (ensemble_fields, priors)

    return lax.fori_loop(0, obs_cells.shape[0], serial_step, (ensemble_fields, priors))


def local(
    tracer, east_speed, north_speed, diffusivity, obs_cell, tile_offset, obs_value, obs_error
):
    members_here, depth_levels, own_cols, whole_grid_lines = tracer.shape
    own_rows = whole_grid_lines // lax.axis_size("member")
    col_start = lax.axis_index("domain") * own_cols
    row_start = lax.axis_index("member") * own_rows
    stacked = jnp.concatenate([tracer, east_speed[:, None], north_speed[:, None]], axis=1)
    local_rates = lax.dynamic_slice_in_dim(
        diffusivity, lax.axis_index("member") * members_here, members_here
    )
    halo_padded = padded(stacked, (("domain", 2),), 1)
    halo_padded = jnp.pad(halo_padded, ((0, 0), (0, 0), (0, 0), (1, 1)))
    advance_prediction = concentration_change(
        halo_padded,
        depth_levels,
        local_rates,
        closed_edge_flags(whole_grid_lines, whole_grid_lines),
    )
    ensemble_fields = lax.all_to_all(
        advance_prediction, "member", split_axis=3, concat_axis=0, tiled=True
    )
    for batch_num in range(obs_cell.shape[0]):
        priors = block_priors(ensemble_fields, obs_cell[batch_num], col_start, row_start)
        ensemble_fields, priors = filter_batch(
            ensemble_fields,
            priors,
            obs_cell[batch_num],
            tile_offset[batch_num],
            obs_value[batch_num],
            obs_error[batch_num],
            col_start,
            row_start,
        )
    return ensemble_fields


def solution(mesh):
    placed = (
        P("member", None, "domain", None),
        P("member", "domain", None),
        P("member", "domain", None),
        P(),
        P(),
        P(),
        P(),
        P(),
    )
    return jax.shard_map(
        local,
        mesh=mesh,
        in_specs=placed,
        out_specs=P(None, None, "domain", "member"),
        check_vma=False,
    )
```

profile of v0, /device:TPU:217, one launch (start us, length us, event | category | flops | bytes accessed | tf_op | source)
XLA Modules:
  0.0 2288.2 jit_solution(14950816539915794511)
XLA Ops:
  17.4 7.2 copy.37
  24.6 9.8 reshape.277
  34.4 6.7 all-to-all-start
  41.3 21.3 all-to-all-done
  63.1 4.4 reduce.2
  67.5 8.7 reshape.278
  76.2 7.4 copy.38
  88.7 73.2 %psum.14 = f32[64,64]{1,0:T(8,128)S(1)} all-reduce(f32[64,64]{1,0:T(8,128)S(1)} %fusion.32), channel_id=1, replica_groups=mesh['member'=8,'domain'=32] {'member','domain'}, use_global_device_ids=true, to_apply=%region_0.2 | all-reduce | flops 4096 | bytes 32768 | tf_op jit(solution)/shard_map/psum | solution.py:112
  161.9 864.4 %while.42 = (s32[]{:T(128)}, f32[64,3,16,128]{3,2,1,0:T(8,128)S(1)}, f32[64,64]{1,0:T(8,128)S(1)}, s32[64,2]{0,1:T(2,128)S(1)}, s32[]{:T(128)}, /*index=5*/s32[]...) while((s32[]{:T(128)}, ...), condition=%wide.region_6.8_spmd.clone.clone, body=%wide.region_1.7_spmd.clone.clone.sunk | while | flops 2821999 | bytes 5609359 | solution.py:173
  171.2 3.4 fusion.49
  183.9 3.4 fusion.49
  196.6 3.4 fusion.49
  209.3 3.4 fusion.49
  222.0 3.4 fusion.49
  234.8 3.4 fusion.49
  247.5 50.3 %conditional.8 = (f32[64,3,16,128]{3,2,1,0:T(8,128)S(1)}) conditional(s32[]{:T(128)} %convert_element_type.106, f32[64,3,16,128]{3,2,1,0:T(8,128)S(1)} %get-tuple-element.1062, (s32[]{:T(128)}, s32[]{:T(128)}, f32[64,3,16,128]{3,2,1,0:T(8,128)S(1)}, s32[]{:T(128)}, s32[3]{0:T(128)S(1)}, /*index=5*/s32[]{:T(128)}, s32[]{:T(128)}, s32[]{:T(128)}, ...), branch_computations={%region_4.5_spmd, %region_5.6_spmd} | conditional | flops 2762716 | bytes 5556464 | solution.py:158
  255.3 42.5 %dynamic_update_slice.6 = f32[64,3,16,128]{3,2,1,0:T(8,128)S(1)} dynamic-update-slice(f32[64,3,16,128]{3,2,1,0:T(8,128)S(1)} %get-tuple-element.612, f32[64,3,16,64]{3,2,1,0:T(8,128)S(1)} %multiply_add_fusion, s32[]{:T(128)} %constant.274.clone, s32[]{:T(128)} %constant.274.clone, s32[]{:T(128)} %constant.274.clone, s32[]{:T(128)S(6)} %min.23) | dynamic-update-slice | bytes 1572868 | tf_op jit(solution)/shard_map/while/body/eval_jaxpr/cond/branch_1_fun/dynamic_update_slice | solution.py:151
  297.8 3.4 fusion.49
  310.5 3.4 fusion.49
  323.2 3.4 fusion.49
  335.9 3.4 fusion.49
  348.7 3.4 fusion.49
  361.4 3.4 fusion.49
  374.1 3.4 fusion.49
  386.8 3.4 fusion.49
  399.5 3.4 fusion.49
  412.3 3.4 fusion.49
  425.0 3.4 fusion.49
  437.7 3.4 fusion.49
  450.4 3.4 fusion.49
  463.1 3.4 fusion.49
  475.9 3.4 fusion.49
  488.6 3.4 fusion.49
  501.3 3.4 fusion.49
  514.0 3.4 fusion.49
  526.7 3.4 fusion.49
  539.5 3.4 fusion.49
  552.2 3.4 fusion.49
  564.9 3.4 fusion.49
  577.6 3.4 fusion.49
  590.3 3.4 fusion.49
  603.1 3.4 fusion.49
  615.8 3.4 fusion.49
  628.5 3.4 fusion.49
  641.2 3.4 fusion.49
  654.0 3.4 fusion.49
  666.7 3.4 fusion.49
  679.4 3.4 fusion.49
  692.1 3.4 fusion.49
  704.8 3.4 fusion.49
  717.6 3.4 fusion.49
  730.3 3.4 fusion.49
  743.0 3.4 fusion.49
  755.7 3.4 fusion.49
  1031.1 240.6 %psum.15 = f32[64,64]{1,0:T(8,128)S(1)} all-reduce(f32[64,64]{1,0:T(8,128)S(1)} %fusion.31), channel_id=1, replica_groups=mesh['member'=8,'domain'=32] {'member','domain'}, use_global_device_ids=true, to_apply=%region_7.9 | all-reduce | flops 4096 | bytes 32768 | tf_op jit(solution)/shard_map/psum | solution.py:112
  1271.7 1015.3 %while.43 = (s32[]{:T(128)}, f32[64,3,16,128]{3,2,1,0:T(8,128)S(1)}, f32[64,64]{1,0:T(8,128)S(1)}, s32[64,2]{0,1:T(2,128)S(1)}, s32[]{:T(128)}, /*index=5*/s32[]...) while((s32[]{:T(128)}, ...), condition=%wide.region_13.15_spmd.clone.clone, body=%wide.region_8.14_spmd.clone.clone.sunk | while | flops 2821999 | bytes 5609359 | solution.py:173
  1535.4 50.3 %conditional.9 = (f32[64,3,16,128]{3,2,1,0:T(8,128)S(1)}) conditional(s32[]{:T(128)} %convert_element_type.109, f32[64,3,16,128]{3,2,1,0:T(8,128)S(1)} %get-tuple-element.1116, (s32[]{:T(128)}, s32[]{:T(128)}, f32[64,3,16,128]{3,2,1,0:T(8,128)S(1)}, s32[]{:T(128)}, s32[3]{0:T(128)S(1)}, /*index=5*/s32[]{:T(128)}, s32[]{:T(128)}, s32[]{:T(128)}, ...), branch_computations={%region_11.12_spmd, %region_12.13_spmd} | conditional | flops 2762716 | bytes 5556464 | solution.py:158
  1543.2 42.5 %dynamic_update_slice.7 = f32[64,3,16,128]{3,2,1,0:T(8,128)S(1)} dynamic-update-slice(f32[64,3,16,128]{3,2,1,0:T(8,128)S(1)} %get-tuple-element.639, f32[64,3,16,64]{3,2,1,0:T(8,128)S(1)} %multiply_add_fusion.1, s32[]{:T(128)} %constant.298.clone, s32[]{:T(128)} %constant.298.clone, s32[]{:T(128)} %constant.298.clone, s32[]{:T(128)S(6)} %min.24) | dynamic-update-slice | bytes 1572868 | tf_op jit(solution)/shard_map/while/body/eval_jaxpr/cond/branch_1_fun/dynamic_update_slice | solution.py:151
  1878.3 50.3 %conditional.9 = (f32[64,3,16,128]{3,2,1,0:T(8,128)S(1)}) conditional(s32[]{:T(128)} %convert_element_type.109, f32[64,3,16,128]{3,2,1,0:T(8,128)S(1)} %get-tuple-element.1116, (s32[]{:T(128)}, s32[]{:T(128)}, f32[64,3,16,128]{3,2,1,0:T(8,128)S(1)}, s32[]{:T(128)}, s32[3]{0:T(128)S(1)}, /*index=5*/s32[]{:T(128)}, s32[]{:T(128)}, s32[]{:T(128)}, ...), branch_computations={%region_11.12_spmd, %region_12.13_spmd} | conditional | flops 2762716 | bytes 5556464 | solution.py:158
  1886.1 42.5 %dynamic_update_slice.7 = f32[64,3,16,128]{3,2,1,0:T(8,128)S(1)} dynamic-update-slice(f32[64,3,16,128]{3,2,1,0:T(8,128)S(1)} %get-tuple-element.639, f32[64,3,16,64]{3,2,1,0:T(8,128)S(1)} %multiply_add_fusion.1, s32[]{:T(128)} %constant.298.clone, s32[]{:T(128)} %constant.298.clone, s32[]{:T(128)} %constant.298.clone, s32[]{:T(128)S(6)} %min.24) | dynamic-update-slice | bytes 1572868 | tf_op jit(solution)/shard_map/while/body/eval_jaxpr/cond/branch_1_fun/dynamic_update_slice | solution.py:151
  1966.7 50.3 %conditional.9 = (f32[64,3,16,128]{3,2,1,0:T(8,128)S(1)}) conditional(s32[]{:T(128)} %convert_element_type.109, f32[64,3,16,128]{3,2,1,0:T(8,128)S(1)} %get-tuple-element.1116, (s32[]{:T(128)}, s32[]{:T(128)}, f32[64,3,16,128]{3,2,1,0:T(8,128)S(1)}, s32[]{:T(128)}, s32[3]{0:T(128)S(1)}, /*index=5*/s32[]{:T(128)}, s32[]{:T(128)}, s32[]{:T(128)}, ...), branch_computations={%region_11.12_spmd, %region_12.13_spmd} | conditional | flops 2762716 | bytes 5556464 | solution.py:158
  1974.6 42.5 %dynamic_update_slice.7 = f32[64,3,16,128]{3,2,1,0:T(8,128)S(1)} dynamic-update-slice(f32[64,3,16,128]{3,2,1,0:T(8,128)S(1)} %get-tuple-element.639, f32[64,3,16,64]{3,2,1,0:T(8,128)S(1)} %multiply_add_fusion.1, s32[]{:T(128)} %constant.298.clone, s32[]{:T(128)} %constant.298.clone, s32[]{:T(128)} %constant.298.clone, s32[]{:T(128)S(6)} %min.24) | dynamic-update-slice | bytes 1572868 | tf_op jit(solution)/shard_map/while/body/eval_jaxpr/cond/branch_1_fun/dynamic_update_slice | solution.py:151
  2106.1 50.3 %conditional.9 = (f32[64,3,16,128]{3,2,1,0:T(8,128)S(1)}) conditional(s32[]{:T(128)} %convert_element_type.109, f32[64,3,16,128]{3,2,1,0:T(8,128)S(1)} %get-tuple-element.1116, (s32[]{:T(128)}, s32[]{:T(128)}, f32[64,3,16,128]{3,2,1,0:T(8,128)S(1)}, s32[]{:T(128)}, s32[3]{0:T(128)S(1)}, /*index=5*/s32[]{:T(128)}, s32[]{:T(128)}, s32[]{:T(128)}, ...), branch_computations={%region_11.12_spmd, %region_12.13_spmd} | conditional | flops 2762716 | bytes 5556464 | solution.py:158
  2113.9 42.5 %dynamic_update_slice.7 = f32[64,3,16,128]{3,2,1,0:T(8,128)S(1)} dynamic-update-slice(f32[64,3,16,128]{3,2,1,0:T(8,128)S(1)} %get-tuple-element.639, f32[64,3,16,64]{3,2,1,0:T(8,128)S(1)} %multiply_add_fusion.1, s32[]{:T(128)} %constant.298.clone, s32[]{:T(128)} %constant.298.clone, s32[]{:T(128)} %constant.298.clone, s32[]{:T(128)S(6)} %min.24) | dynamic-update-slice | bytes 1572868 | tf_op jit(solution)/shard_map/while/body/eval_jaxpr/cond/branch_1_fun/dynamic_update_slice | solution.py:151
  (1450 shorter events, 751.6 us)
Async XLA Ops:
  0.0 2.4 copy-start.3
  0.0 2.4 copy-start.2
  3.1 1.9 copy-start.8
  3.1 4.1 collective-permute-start
  4.9 5.6 collective-permute-start.1
  14.7 1.4 copy-start.1
  34.4 6.8 copy-start.4
  34.4 6.8 copy-start.5
  34.4 6.9 copy-start.6
  34.4 6.9 copy-start.7
  34.4 28.2 %all-to-all-start = ((f32[8,1,49152]{2,1,0:T(1,128)}), f32[8,1,49152]{2,1,0:T(1,128)S(1)}, u32[]{:S(2)}, u32[]{:S(2)}) async-start(f32[8,1,49152]{2,1,0:T(1,128)} %reshape.277), calls=%async_computation | async-start | bytes 3145728 | tf_op jit(solution)/shard_map/all_to_all | solution.py:195
  2287.0 1.2 copy-start
where the time goes:
time: 2310 us; the launch traced here: 2290 us
  loops' own time  802 us (35%)
  local copies, waits for them, and re-layouts  502 us (22%)
  matrix products  435 us (19%)
  blocking collectives  314 us (14%)
  other arithmetic  199 us (9%)
  waiting for transfers between devices  26.8 us (1%)
    another operation x2, loops' own time, filter_batch(): lax.fori_loop(0, obs_cells.shape[0], serial_step, (ensemble_fields, priors))  790 us
    dot_general x128, matrix products, update_priors(): obs_cov = jnp.dot(priors, spread, precision=lax.Precision.HIGHEST)  429 us
    psum x2, blocking collectives, block_priors(): return lax.psum(picked, ('member', 'domain'))  314 us
    dynamic_update_slice x5, local copies, waits for them, and re-layouts, apply_update(): lax.dynamic_update_slice(block, window, (zero_index, zero_index, zero_ind...  212 us
    dynamic_slice x128, local copies, waits for them, and re-layouts, serial_step(): obs_row = obs_cells[obs_index, 2]  87.3 us
    reduce_sum x128, other arithmetic, innovation(): average = jnp.mean(current)  79.1 us
    reduce_sum x128, other arithmetic, innovation(): variance = jnp.sum(spread * spread) / (members - 1)  78.1 us
    dynamic_slice x128, local copies, waits for them, and re-layouts, innovation(): correction = obs_values[obs_index] - average - reduction * spread  75.4 us
  transfers between devices with their start and end apart: 3, of which 3 were waited for; matrix products, arithmetic and copies ran while one was open for 0% of the time, Pallas kernels for 0%

commit v1 on v0

v1 whole, which is shorter than its diff:
```python
import functools

import jax
import jax.numpy as jnp
from jax import lax
from jax.experimental import pallas as pl
from jax.experimental.pallas import tpu as pltpu
from jax.sharding import PartitionSpec as P

TILE_X = 32
TILE_Y = 64
LANES = 128
NONE = 999.0
LAST = 0x7FFFFFFF
PLANES = 5
VMEM_BYTES = 32 * 1024 * 1024
WHOLE_VMEM = 64 * 1024 * 1024 - 65536


def lane_row(ref, *index):
    return jnp.concatenate([ref[(*index, slice(0, 1))], ref[(*index, slice(1, 2))]], axis=1)


def copies(pairs, sems):
    made = [pltpu.make_async_copy(src, dst, sems.at[i]) for i, (src, dst) in enumerate(pairs)]
    for one in made:
        one.start()
    return made


def face_flux(u_low, u_high, q_low, q_high, rate):
    face = 0.5 * (u_low + u_high)
    return (
        jnp.maximum(face, 0.0) * q_low + jnp.minimum(face, 0.0) * q_high - rate * (q_high - q_low)
    )


def prepare_kernel(
    domains, cell_ref, tile_ref, rate_ref, tracer_hbm, east_hbm, north_hbm,
    low_ref, high_ref, picked_ref, meta_ref, tracer_ref, east_ref, north_ref, sems,
):
    members, levels, cols, length = tracer_ref.shape
    loads = copies(
        [(tracer_hbm, tracer_ref), (east_hbm, east_ref), (north_hbm, north_ref)], sems
    )
    domain = lax.axis_index("domain")
    me = lax.axis_index("member")
    col0 = domain * cols
    width = domains * cols
    level = lane_row(cell_ref, 0)
    x = lane_row(cell_ref, 1)
    y = lane_row(cell_ref, 2)
    ox = jnp.concatenate([tile_ref[0, 0:1], tile_ref[1, 0:1]], axis=1)
    oy = jnp.concatenate([tile_ref[0, 1:2], tile_ref[1, 1:2]], axis=1)
    lane = lax.broadcasted_iota(jnp.int32, (1, LANES), 1)
    zero = jnp.zeros((3, LANES), jnp.int32)
    meta_ref[...] = jnp.concatenate([level, x, y, ox, oy, zero], axis=0)
    near = (x >= col0) & (x < col0 + cols)
    before = jnp.where(col0 == 0, width, col0) - 1
    after = jnp.where(col0 + cols == width, 0, col0 + cols)
    near = near | (x == before) | (x == after)
    keys = jnp.where(near, (lane << 21) + (level << 19) + (x << 10) + y, LAST)
    picked_ref[...] = jnp.zeros_like(picked_ref)
    for one in loads:
        one.wait()
    for i, edge in ((0, low_ref), (cols - 1, high_ref)):
        edge[:, :levels] = tracer_ref[:, :, i]
        edge[:, levels] = east_ref[:, i]

    sub = lax.broadcasted_iota(jnp.int32, (members, LANES), 0)
    lanes = lax.broadcasted_iota(jnp.int32, (members, LANES), 1)
    rates = jnp.zeros((members, LANES), jnp.float32)
    for m in range(members):
        rates = jnp.where(sub == m, rate_ref[me * members + m], rates)

    def pick(key):
        k = key >> 21
        l = (key >> 19) & 3
        col = (key >> 10) & 511
        row = key & 1023
        here = col - col0
        own = (here >= 0) & (here < cols)

        def fetch(ref, lead, i, j):
            i = jnp.clip(i, 0, cols - 1)
            j = jnp.clip(j, 0, length - 1)
            first = pl.multiple_of((i >> 3) << 3, 8)
            start = pl.multiple_of((j >> 7) << 7, LANES)
            rows = jnp.zeros((members, LANES), jnp.float32)
            for m in range(members):
                tile = ref[(m, *lead, pl.ds(first, 8), pl.ds(start, LANES))]
                rows = jnp.where(sub == m, pltpu.roll(tile, (m - i) & 7, 0), rows)
            return pltpu.roll(rows, (k - (j & 127) + LANES) & 127, 1)

        mine = lanes == k

        def put(plane, value):
            at = slice(plane * members, (plane + 1) * members)
            picked_ref[at] = jnp.where(mine, value, picked_ref[at])

        @pl.when(own)
        def _():
            q = fetch(tracer_ref, (l,), here, row)
            u = fetch(east_ref, (), here, row)
            v = fetch(north_ref, (), here, row)
            south = face_flux(
                fetch(north_ref, (), here, row - 1), v, fetch(tracer_ref, (l,), here, row - 1), q, rates
            )
            north = face_flux(
                v, fetch(north_ref, (), here, row + 1), q, fetch(tracer_ref, (l,), here, row + 1), rates
            )
            low = face_flux(
                fetch(east_ref, (), here - 1, row), u, fetch(tracer_ref, (l,), here - 1, row), q, rates
            )
            high = face_flux(
                u, fetch(east_ref, (), here + 1, row), q, fetch(tracer_ref, (l,), here + 1, row), rates
            )
            south = jnp.where(row == 0, 0.0, south)
            north = jnp.where(row == length - 1, 0.0, north)
            low = jnp.where(here == 0, 0.0, low)
            high = jnp.where(here == cols - 1, 0.0, high)
            put(0, q - (high - low) - (north - south))
            put(1, q)
            put(2, u)

        @pl.when(jnp.logical_not(own))
        def _():
            there = jnp.where(col == before, 0, cols - 1)
            put(3, fetch(tracer_ref, (l,), there, row))
            put(4, fetch(east_ref, (), there, row))

    def step(key):
        pick(key)
        return jnp.min(jnp.where(keys > key, keys, LAST))

    lax.while_loop(lambda key: key < LAST, step, jnp.min(keys))


def prepare(cells, tiles, rates, tracer, east, north, domains):
    members, levels, cols, length = tracer.shape
    vmem = pl.BlockSpec(memory_space=pltpu.VMEM)
    hbm = pl.BlockSpec(memory_space=pltpu.HBM)
    edge = jax.ShapeDtypeStruct((members, levels + 1, length), jnp.float32)
    return pl.pallas_call(
        functools.partial(prepare_kernel, domains),
        out_shape=[
            edge,
            edge,
            jax.ShapeDtypeStruct((PLANES * members, LANES), jnp.float32),
            jax.ShapeDtypeStruct((8, LANES), jnp.int32),
        ],
        in_specs=[vmem, vmem, pl.BlockSpec(memory_space=pltpu.SMEM), hbm, hbm, hbm],
        out_specs=[vmem] * 4,
        scratch_shapes=[
            pltpu.VMEM(tracer.shape, jnp.float32),
            pltpu.VMEM(east.shape, jnp.float32),
            pltpu.VMEM(north.shape, jnp.float32),
            pltpu.SemaphoreType.DMA((3,)),
        ],
        compiler_params=pltpu.CompilerParams(vmem_limit_bytes=WHOLE_VMEM),
        cost_estimate=pl.CostEstimate(flops=1_000_000, bytes_accessed=3_000_000, transcendentals=0),
        name="prepare",
    )(cells, tiles, rates, tracer, east, north)


def forecast_kernel(
    rate_ref, below_ref, above_ref, tracer_ref, east_ref, north_ref, out_ref
):
    members, levels, cols, length = tracer_ref.shape
    bands = out_ref.shape[0]
    me = lax.axis_index("member")
    lane = lax.broadcasted_iota(jnp.int32, (cols, LANES), 1)

    def sides(read, d):
        here = read(d)
        left = jnp.where(lane == LANES - 1, read(d - 1), here) if d else here
        right = jnp.where(lane == 0, read(d + 1), here) if d < bands - 1 else here
        return (pltpu.roll(left, 1, 1), here, pltpu.roll(right, LANES - 1, 1))

    def weights(low, high, rate):
        face = 0.5 * (low + high)
        return (jnp.maximum(face, 0.0) + rate, jnp.minimum(face, 0.0) - rate)

    def member(g, carry):
        rate = rate_ref[me * members + g]
        for d in range(bands):
            at = lambda i: pl.ds(i * LANES, LANES)
            u = east_ref[g, :, at(d)]
            u_low = jnp.concatenate([below_ref[g, levels : levels + 1, at(d)], u[:-1]], axis=0)
            behind, ahead = weights(u_low, u, rate)
            behind_last, ahead_last = weights(
                u[-1:], above_ref[g, levels : levels + 1, at(d)], rate
            )
            v_left, v, v_right = sides(lambda i: north_ref[g, :, at(i)], d)
            south_low, south_high = weights(v_left, v, rate)
            north_low, north_high = weights(v, v_right, rate)
            if d == 0:
                south_low = jnp.where(lane == 0, 0.0, south_low)
                south_high = jnp.where(lane == 0, 0.0, south_high)
            if d == bands - 1:
                north_low = jnp.where(lane == LANES - 1, 0.0, north_low)
                north_high = jnp.where(lane == LANES - 1, 0.0, north_high)
            for l in range(levels):
                q_left, q, q_right = sides(lambda i: tracer_ref[g, l, :, at(i)], d)
                q_low = jnp.concatenate([below_ref[g, l : l + 1, at(d)], q[:-1]], axis=0)
                flux = behind * q_low + ahead * q
                flux_last = behind_last * q[-1:] + ahead_last * above_ref[g, l : l + 1, at(d)]
                flux_up = jnp.concatenate([flux[1:], flux_last], axis=0)
                south = south_low * q_left + south_high * q
                north = north_low * q + north_high * q_right
                out_ref[d, g, l] = q - (flux_up - flux) - (north - south)
        return carry

    lax.fori_loop(0, members, member, 0)


def forecast(rates, below, above, tracer, east, north, bands):
    members, levels, cols, length = tracer.shape
    vmem = pl.BlockSpec(memory_space=pltpu.VMEM)
    return pl.pallas_call(
        forecast_kernel,
        out_shape=jax.ShapeDtypeStruct((bands, members, levels, cols, LANES), jnp.float32),
        in_specs=[pl.BlockSpec(memory_space=pltpu.SMEM)] + [vmem] * 5,
        out_specs=vmem,
        compiler_params=pltpu.CompilerParams(vmem_limit_bytes=VMEM_BYTES),
        cost_estimate=pl.CostEstimate(
            flops=16_000_000, bytes_accessed=4_500_000, transcendentals=0
        ),
        name="forecast",
    )(rates, below, above, tracer, east, north)


def innovations(priors, values, errors):
    members = priors.shape[0]
    average = jnp.sum(priors, axis=0, keepdims=True) / members
    spread = priors - average
    variance = jnp.sum(spread * spread, axis=0, keepdims=True) / (members - 1)
    divisor = variance + errors
    reduction = 1.0 / (1.0 + jnp.sqrt(errors / divisor))
    factor = 1.0 / ((members - 1) * divisor)
    return (spread, values - average, reduction, factor)


def solve_kernel(prior_ref, meta_ref, value_ref, error_ref, out_ref):
    members, total = prior_ref.shape
    meta = meta_ref[...].astype(jnp.float32)
    across = jnp.concatenate(
        [meta, jnp.zeros((total - meta.shape[0], total), jnp.float32)], axis=0
    ).T
    level_j, x_j, y_j, ox_j, oy_j = (across[:, i : i + 1] for i in range(5))
    level_k, x_k, y_k = (meta[i : i + 1] for i in range(3))
    j_ids = lax.broadcasted_iota(jnp.int32, (total, total), 0)
    k_ids = lax.broadcasted_iota(jnp.int32, (total, total), 1)
    source = j_ids.astype(jnp.float32)
    taper_x = jnp.where(
        (x_k >= ox_j) & (x_k < ox_j + TILE_X), 1.0 - jnp.abs(x_k - x_j) / TILE_X, 0.0
    )
    taper_y = jnp.where(
        (y_k >= oy_j) & (y_k < oy_j + TILE_Y), 1.0 - jnp.abs(y_k - y_j) / TILE_Y, 0.0
    )
    weight = jnp.where(level_j == level_k, 1.0, 0.5) * taper_x * taper_y
    weight = jnp.where(j_ids < k_ids, weight, 0.0)
    pending = jnp.where(weight != 0.0, source, -1.0)
    values = lane_row(value_ref)
    errors = lane_row(error_ref)

    def following(done):
        return jnp.min(jnp.where(pending > done, pending, NONE), axis=0, keepdims=True)

    def step(carry):
        priors, nxt, left = carry
        spread, offset, reduction, factor = innovations(priors, values, errors)
        final = jnp.where(nxt == NONE, 1.0, 0.0)
        table = jnp.concatenate(
            [spread, offset, reduction, factor, final, jnp.zeros((12, total), jnp.float32)], axis=0
        )
        high = table.astype(jnp.bfloat16)
        rest = table - high.astype(jnp.float32)
        middle = rest.astype(jnp.bfloat16)
        low = (rest - middle.astype(jnp.float32)).astype(jnp.bfloat16)
        chosen = source == nxt
        pick = jnp.where(chosen, 1.0, 0.0).astype(jnp.bfloat16)
        dot = lambda part: jnp.dot(part, pick, preferred_element_type=jnp.float32)
        got = dot(high) + dot(middle) + dot(low)
        their_spread = got[:members]
        their_offset, their_reduction, their_factor, ready = (
            got[members + i : members + i + 1] for i in range(4)
        )
        rho = jnp.sum(jnp.where(chosen, weight, 0.0), axis=0, keepdims=True)
        covariance = jnp.sum(priors * their_spread, axis=0, keepdims=True)
        go = ready > 0.5
        scale = jnp.where(go, rho * covariance * their_factor, 0.0)
        priors = priors + scale * (their_offset - their_reduction * their_spread)
        done = jnp.where(go, nxt, nxt - 0.5)
        nxt = following(done)
        return (priors, nxt, jnp.min(nxt))

    nxt = following(jnp.full((1, total), -1.0, jnp.float32))
    priors, _, _ = lax.while_loop(
        lambda carry: carry[2] < NONE, step, (prior_ref[...], nxt, jnp.min(nxt))
    )
    spread, offset, reduction, factor = innovations(priors, values, errors)
    out_ref[0] = spread * factor
    out_ref[1] = offset - reduction * spread


def solve_filter(priors, meta, values, errors):
    vmem = pl.BlockSpec(memory_space=pltpu.VMEM)
    return pl.pallas_call(
        solve_kernel,
        out_shape=jax.ShapeDtypeStruct((2, *priors.shape), jnp.float32),
        in_specs=[vmem] * 4,
        out_specs=vmem,
        name="solve_filter",
    )(priors, meta, values, errors)


def apply_kernel(
    local_members, meta_ref, lanes_ref, table_ref, in_ref, out_ref, work, gain, sems_in, sems_out
):
    members, levels, cols, rows = work.shape
    part = 8
    parts = cols // part
    loads = copies(
        [
            (in_ref.at[:, l, pl.ds(g * part, part)], work.at[:, l, pl.ds(g * part, part)])
            for g in range(parts)
            for l in range(levels)
        ],
        sems_in,
    )
    me = lax.axis_index("member")
    base = lax.axis_index("domain") * cols
    row0 = me * rows
    lane = lax.broadcasted_iota(jnp.int32, (1, LANES), 1)
    ox = lanes_ref[3:4]
    oy = lanes_ref[4:5]
    in_rows = (oy < row0 + rows) & (oy + TILE_Y > row0)

    def taper(position, centre, first, span):
        inside = (position >= first) & (position < first + span)
        return jnp.where(inside, 1.0 - jnp.abs(position - centre).astype(jnp.float32) / span, 0.0)

    def member_row(m):
        return ((m // local_members) ^ me) * local_members + m % local_members

    stores = []
    for g in range(parts):
        for one in loads[g * levels : (g + 1) * levels]:
            one.wait()
        col0 = base + g * part
        keys = jnp.where(in_rows & (ox < col0 + part) & (ox + TILE_X > col0), lane, LAST)
        col_ids = col0 + lax.broadcasted_iota(jnp.int32, (part, rows), 0)
        row_ids = row0 + lax.broadcasted_iota(jnp.int32, (part, rows), 1)
        band = pl.ds(g * part, part)

        def update(k, keys=keys, col_ids=col_ids, row_ids=row_ids, band=band):
            shift = (LANES - k) & 127
            for i in range(2):
                column = pltpu.roll(table_ref[i], shift, 1)[:, 0:1]
                gain[i] = jnp.broadcast_to(column, (members, LANES))
            weight = taper(col_ids, meta_ref[1, k], meta_ref[3, k], TILE_X) * taper(
                row_ids, meta_ref[2, k], meta_ref[4, k], TILE_Y
            )
            sums = [[None, None] for _ in range(levels)]
            for m in range(members):
                s = gain[0, pl.ds(member_row(m), 1)]
                for l in range(levels):
                    term = work[m, l, band] * s
                    old = sums[l][m % 2]
                    sums[l][m % 2] = term if old is None else old + term
            scale = []
            for l in range(levels):
                vertical = jnp.where(meta_ref[0, k] == l, 1.0, 0.5)
                scale.append(vertical * weight * (sums[l][0] + sums[l][1]))
            for m in range(members):
                c = gain[1, pl.ds(member_row(m), 1)]
                for l in range(levels):
                    work[m, l, band] = work[m, l, band] + scale[l] * c
            return jnp.min(jnp.where(keys > k, keys, LAST))

        lax.while_loop(lambda k: k < LAST, update, jnp.min(keys))
        for l in range(levels):
            one = pltpu.make_async_copy(
                work.at[:, l, band], out_ref.at[:, l, band], sems_out.at[g * levels + l]
            )
            one.start()
            stores.append(one)
    for one in stores:
        one.wait()


def apply_updates(meta, table, block, local_members):
    members, levels, cols, rows = block.shape
    vmem = pl.BlockSpec(memory_space=pltpu.VMEM)
    some = pl.BlockSpec(memory_space=pl.ANY)
    count = levels * cols // 8
    return pl.pallas_call(
        functools.partial(apply_kernel, local_members),
        out_shape=jax.ShapeDtypeStruct(block.shape, jnp.float32),
        in_specs=[pl.BlockSpec(memory_space=pltpu.SMEM), vmem, vmem, some],
        out_specs=some,
        scratch_shapes=[
            pltpu.VMEM(block.shape, jnp.float32),
            pltpu.VMEM((2, members, LANES), jnp.float32),
            pltpu.SemaphoreType.DMA((count,)),
            pltpu.SemaphoreType.DMA((count,)),
        ],
        compiler_params=pltpu.CompilerParams(vmem_limit_bytes=WHOLE_VMEM),
        name="apply_updates",
    )(meta, meta, table, block)


def exchange(array, axis, peers, reach):
    return lax.ppermute(array, axis, [(i, i ^ reach) for i in range(peers)])


def finish_priors(picked, meta, rates, cols):
    whole, q, u, q_far, u_far = jnp.split(picked, PLANES, axis=0)
    place = meta[1:2] & (cols - 1)
    rate = rates[:, None]
    low = face_flux(u_far, u, q_far, q, rate)
    high = face_flux(u, u_far, q, q_far, rate)
    return whole + jnp.where(place == 0, low, 0.0) - jnp.where(place == cols - 1, high, 0.0)


def local(
    tracer, east_speed, north_speed, diffusivity, obs_cell, tile_offset, obs_value, obs_error
):
    members, levels, cols, length = tracer.shape
    bands = lax.axis_size("member")
    domains = lax.axis_size("domain")
    cells = obs_cell.transpose(2, 0, 1)
    tiles = tile_offset.transpose(0, 2, 1)
    rates = lax.dynamic_slice_in_dim(diffusivity, lax.axis_index("member") * members, members)
    low, high, picked, meta = prepare(
        cells, tiles, diffusivity, tracer, east_speed, north_speed, domains
    )
    up = [(i, (i + 1) % domains) for i in range(domains)]
    down = [(j, i) for i, j in up]
    below = lax.ppermute(high, "domain", up)
    above = lax.ppermute(low, "domain", down)
    for reach in (1, 2):
        picked = picked + exchange(picked, "domain", domains, reach)
    below, above, picked = lax.optimization_barrier((below, above, picked))
    blocks = forecast(diffusivity, below, above, tracer, east_speed, north_speed, bands)
    picked = picked + exchange(picked, "domain", domains, 4)
    blocks, picked = lax.optimization_barrier((blocks, picked))
    block = lax.all_to_all(blocks, "member", split_axis=0, concat_axis=0, tiled=True)
    block = block.reshape(bands * members, levels, cols, length // bands)
    reach = 8
    while reach < domains:
        picked = picked + exchange(picked, "domain", domains, reach)
        reach *= 2
    priors = finish_priors(picked, meta, rates, cols)
    reach = 1
    while reach < bands:
        priors = jnp.concatenate([priors, exchange(priors, "member", bands, reach)], axis=0)
        reach *= 2
    table = solve_filter(priors, meta, obs_value, obs_error)
    return apply_updates(meta, table, block, members)


def solution(mesh):
    placed = (
        P("member", None, "domain", None),
        P("member", "domain", None),
        P("member", "domain", None),
        P(),
        P(),
        P(),
        P(),
        P(),
    )
    return jax.shard_map(
        local,
        mesh=mesh,
        in_specs=placed,
        out_specs=P(None, None, "domain", "member"),
        check_vma=False,
    )
```

time: 2310 us -> 72.1 us (0.03)
  the two profiles are of different devices: /device:TPU:217 before, /device:TPU:74 now
where the time goes in v1:
time: 72.1 us; the launch traced here: 72.7 us
  waiting for transfers between devices  27.5 us (38%)
  starting transfers between devices  20.5 us (28%)
  Pallas kernels  18.2 us (25%)
  local copies, waits for them, and re-layouts  4.22 us (6%)
  other arithmetic  2.13 us (3%)
    ppermute x8, waiting for transfers between devices, exchange(): return lax.ppermute(array, axis, [(i, i ^ reach) for i in range(peers)])  27.5 us
    ppermute x8, starting transfers between devices, exchange(): return lax.ppermute(array, axis, [(i, i ^ reach) for i in range(peers)])  11.9 us
    all_to_all x1, starting transfers between devices, local(): lax.all_to_all(blocks, 'member', split_axis=0, concat_axis=0, tiled=True)  6.78 us
    pallas_call x1, Pallas kernels, apply_updates(): pl.pallas_call(functools.partial(apply_kernel, local_members), out_shape=...  6.75 us
    pallas_call x1, Pallas kernels, prepare(): pl.pallas_call(functools.partial(prepare_kernel, domains), out_shape=[edg...  5.44 us
    unnamed x10, local copies, waits for them, and re-layouts  4.15 us
    pallas_call x1, Pallas kernels, forecast(): pl.pallas_call(forecast_kernel, out_shape=jax.ShapeDtypeStruct((bands, me...  3.43 us
    pallas_call x1, Pallas kernels, solve_filter(): pl.pallas_call(solve_kernel, out_shape=jax.ShapeDtypeStruct((2, *priors.s...  2.54 us
  transfers between devices with their start and end apart: 11, of which 7 were waited for; matrix products, arithmetic and copies ran while one was open for 3% of the time, Pallas kernels for 8%

profile of v1, /device:TPU:74, one launch (start us, length us, event | category | flops | bytes accessed | tf_op | source)
XLA Modules:
  0.0 72.7 jit_solution(13782550808547647959)
XLA Ops:
  0.0 5.4 %prepare.1 = (f32[8,4,1024]{2,1,0:T(4,128)}, f32[8,4,1024]{2,1,0:T(4,128)}, f32[40,128]{1,0:T(8,128)}, s32[8,128]{1,0:T(8,128)}) custom-call(s32[3,2,64]{2,1,0:T(2,128)} %bitcast.7, s32[2,2,64]{2,1,0:T(2,128)} %bitcast.8, f32[64]{0:T(128)} %rate_ref.3, f32[8,3,16,1024]{3,2,1,0:T(8,128)} %tracer_ref.1, f32[8,16,1024]{2,1,0:T(8,128)} %east_ref.1, ...), custom_call_target="tpu_custom_call" | custom-call | flops 1000000 | bytes 3000000 | tf_op jit(solution)/shard_map/prepare/pallas_call | solution.py:144
  5.5 0.1 collective-permute-start
  5.5 1.7 %collective-permute-start.1 = (f32[8,4,1024]{2,1,0:T(4,128)}, f32[8,4,1024]{2,1,0:T(4,128)S(1)}, u32[]{:S(2)}, u32[]{:S(2)}) collective-permute-start(f32[8,4,1024]{2,1,0:T(4,128)} %get-tuple-element.16), channel_id=1, source_target_pairs={{1,0},{2,1},{3,2},{4,3},{5,4},{6,5},{7,6},{8,7},{9,8},{10,9},{11,1... | collective-permute-start | bytes 393224 | tf_op jit(solution)/shard_map/ppermute | solution.py:442
  7.3 0.0 collective-permute-start.2
  7.3 1.4 %collective-permute-done.2 = f32[40,128]{1,0:T(8,128)S(1)} collective-permute-done((f32[40,128]{1,0:T(8,128)}, f32[40,128]{1,0:T(8,128)S(1)}, u32[]{:S(2)}, u32[]{:S(2)}) %collective-permute-start.2) | collective-permute-done | bytes 20512 | tf_op jit(solution)/shard_map/ppermute | solution.py:415
  8.7 0.7 %add.31 = f32[40,128]{1,0:T(8,128)S(1)} add(f32[40,128]{1,0:T(8,128)} %get-tuple-element.17, f32[40,128]{1,0:T(8,128)S(1)} %collective-permute-done.2) | non-fusion elementwise | flops 5120 | bytes 61440 | tf_op jit(solution)/shard_map/add | solution.py:444
  9.4 0.1 collective-permute-start.3
  9.5 3.9 %collective-permute-done.3 = f32[40,128]{1,0:T(8,128)S(1)} collective-permute-done((f32[40,128]{1,0:T(8,128)S(1)}, f32[40,128]{1,0:T(8,128)S(1)}, u32[]{:S(2)}, u32[]{:S(2)}) %collective-permute-start.3) | collective-permute-done | bytes 20512 | tf_op jit(solution)/shard_map/ppermute | solution.py:415
  13.4 0.0 collective-permute-done.below_ref
  13.4 0.0 collective-permute-done.1.above_ref
  13.4 6.2 %collective-permute-start.4 = (f32[40,128]{1,0:T(8,128)S(1)}, f32[40,128]{1,0:T(8,128)S(1)}, u32[]{:S(2)}, u32[]{:S(2)}) collective-permute-start(f32[40,128]{1,0:T(8,128)S(1)} %add.32), channel_id=1, source_target_pairs={{0,4},{1,5},{2,6},{3,7},{4,0},{5,1},{6,2},{7,3},{8,12},{9,13},{10,... | collective-permute-start | bytes 61448 | tf_op jit(solution)/shard_map/ppermute | solution.py:415
  19.6 0.0 copy-start
  19.6 1.4 %copy-done = f32[8,3,16,1024]{3,2,1,0:T(8,128)S(1)} copy-done((f32[8,3,16,1024]{3,2,1,0:T(8,128)S(1)}, f32[8,3,16,1024]{3,2,1,0:T(8,128)}, u32[]{:S(2)}) %copy-start) | copy-done | bytes 1572888
  21.0 0.0 copy-start.1
  21.0 1.0 %copy-done.1 = f32[8,16,1024]{2,1,0:T(8,128)S(1)} copy-done((f32[8,16,1024]{2,1,0:T(8,128)S(1)}, f32[8,16,1024]{2,1,0:T(8,128)}, u32[]{:S(2)}) %copy-start.1) | copy-done | bytes 524312
  22.0 0.0 copy-start.2
  22.0 1.0 %copy-done.2 = f32[8,16,1024]{2,1,0:T(8,128)S(1)} copy-done((f32[8,16,1024]{2,1,0:T(8,128)S(1)}, f32[8,16,1024]{2,1,0:T(8,128)}, u32[]{:S(2)}) %copy-start.2) | copy-done | bytes 524312
  23.1 0.0 copy-start.3
  23.1 0.7 copy-done.3
  23.7 3.4 %forecast.1 = f32[8,8,3,16,128]{4,3,2,1,0:T(8,128)} custom-call(f32[64]{0:T(128)S(1)} %copy-done.3, f32[8,4,1024]{2,1,0:T(4,128)S(1)} %collective-permute-done.below_ref, f32[8,4,1024]{2,1,0:T(4,128)S(1)} %collective-permute-done.1.above_ref, f32[8,3,16,1024]{3,2,1,0:T(8,128)S(1)} %copy-done, f32[8,16,1024]{2,1,0:T(8,128)S(1)} %copy-done.1, ...), custom_call_target="tpu_custom_call" | custom-call | flops 16000000 | bytes 4500000 | tf_op jit(solution)/shard_map/forecast/pallas_call | solution.py:220
  27.1 0.0 collective-permute-done.4
  27.2 0.0 copy-start.4
  27.2 6.8 %all-to-all-start = ((f32[8,8,3,16,128]{4,3,2,1,0:T(8,128)}), f32[8,8,3,16,128]{4,3,2,1,0:T(8,128)}, u32[]{:S(2)}, u32[]{:S(2)}) async-start(f32[8,8,3,16,128]{4,3,2,1,0:T(8,128)} %forecast.1), calls=%async_computation | async-start | bytes 3145728 | tf_op jit(solution)/shard_map/all_to_all | solution.py:449
  33.9 0.0 collective-permute-start.5
  34.0 4.7 %collective-permute-done.5 = f32[40,128]{1,0:T(8,128)S(1)} collective-permute-done((f32[40,128]{1,0:T(8,128)S(1)}, f32[40,128]{1,0:T(8,128)S(1)}, u32[]{:S(2)}, u32[]{:S(2)}) %collective-permute-start.5) | collective-permute-done | bytes 20512 | tf_op jit(solution)/shard_map/ppermute | solution.py:415
  38.6 0.1 collective-permute-start.6
  38.7 0.7 compare_bitcast_fusion.1
  39.4 0.0 copy-done.4
  39.4 0.1 dynamic_slice.3
  39.5 6.8 %collective-permute-done.6 = f32[40,128]{1,0:T(8,128)S(1)} collective-permute-done((f32[40,128]{1,0:T(8,128)S(1)}, f32[40,128]{1,0:T(8,128)S(1)}, u32[]{:S(2)}, u32[]{:S(2)}) %collective-permute-start.6) | collective-permute-done | bytes 20512 | tf_op jit(solution)/shard_map/ppermute | solution.py:415
  46.3 0.1 fusion.1
  46.4 3.0 %collective-permute-start.7 = (f32[8,128]{1,0:T(8,128)S(1)}, f32[8,128]{1,0:T(8,128)S(1)}, u32[]{:S(2)}, u32[]{:S(2)}) collective-permute-start(f32[8,128]{1,0:T(8,128)S(1)} %fusion.1), channel_id=1, source_target_pairs={{0,32},{32,0},{64,96},{96,64},{128,160},{160,128},{192,224},{224,1... | collective-permute-start | bytes 12296 | tf_op jit(solution)/shard_map/ppermute | solution.py:415
  49.4 4.4 %collective-permute-done.7 = f32[8,128]{1,0:T(8,128)S(1)} collective-permute-done((f32[8,128]{1,0:T(8,128)S(1)}, f32[8,128]{1,0:T(8,128)S(1)}, u32[]{:S(2)}, u32[]{:S(2)}) %collective-permute-start.7) | collective-permute-done | bytes 4128 | tf_op jit(solution)/shard_map/ppermute | solution.py:415
  53.8 0.5 collective-permute-start.8
  54.4 3.1 %collective-permute-done.8 = f32[16,128]{1,0:T(8,128)S(1)} collective-permute-done((f32[16,128]{1,0:T(8,128)S(1)}, f32[16,128]{1,0:T(8,128)S(1)}, u32[]{:S(2)}, u32[]{:S(2)}) %collective-permute-start.8) | collective-permute-done | bytes 8224 | tf_op jit(solution)/shard_map/ppermute | solution.py:415
  57.5 2.1 %collective-permute-start.9 = (f32[32,128]{1,0:T(8,128)S(1)}, f32[32,128]{1,0:T(8,128)S(1)}, u32[]{:S(2)}, u32[]{:S(2)}) collective-permute-start(f32[32,128]{1,0:T(8,128)S(1)} %pad_maximum_fusion.1), channel_id=1, source_target_pairs={{0,128},{32,160},{64,192},{96,224},{128,0},{160,32},{192,64},{224,... | collective-permute-start | bytes 49160 | tf_op jit(solution)/shard_map/ppermute | solution.py:415
  59.6 3.2 %collective-permute-done.9 = f32[32,128]{1,0:T(8,128)S(1)} collective-permute-done((f32[32,128]{1,0:T(8,128)S(1)}, f32[32,128]{1,0:T(8,128)S(1)}, u32[]{:S(2)}, u32[]{:S(2)}) %collective-permute-start.9) | collective-permute-done | bytes 16416 | tf_op jit(solution)/shard_map/ppermute | solution.py:415
  62.7 0.6 pad_maximum_fusion.prior_ref
  63.4 2.5 %solve_filter.1.table_ref = f32[2,64,128]{2,1,0:T(8,128)} custom-call(f32[64,128]{1,0:T(8,128)} %pad_maximum_fusion.prior_ref, s32[8,128]{1,0:T(8,128)} %get-tuple-element.14.meta_ref.lanes_ref, f32[2,64]{1,0:T(2,128)} %value_ref.1, f32[2,64]{1,0:T(2,128)} %error_ref.1), custom_call_target="tpu_custom_call" | custom-call | tf_op jit(solution)/shard_map/solve_filter/pallas_call | solution.py:309
  65.9 0.0 all-to-all-done
  65.9 6.8 %apply_updates.1 = f32[64,3,16,128]{3,2,1,0:T(8,128)} custom-call(s32[8,128]{1,0:T(8,128)} %get-tuple-element.14.meta_ref.lanes_ref, s32[8,128]{1,0:T(8,128)} %get-tuple-element.14.meta_ref.lanes_ref, f32[2,64,128]{2,1,0:T(8,128)} %solve_filter.1.table_ref, f32[64,3,16,128]{3,2,1,0:T(8,128)} %bitcast.4.in_ref), custom_call_target="tpu_custom_call" | custom-call | tf_op jit(solution)/shard_map/apply_updates/pallas_call | solution.py:398
  (6 shorter events, 0.0 us)
Async XLA Ops:
  5.5 7.9 %collective-permute-start = (f32[8,4,1024]{2,1,0:T(4,128)}, f32[8,4,1024]{2,1,0:T(4,128)S(1)}, u32[]{:S(2)}, u32[]{:S(2)}) collective-permute-start(f32[8,4,1024]{2,1,0:T(4,128)} %get-tuple-element.15), channel_id=1, source_target_pairs={{0,1},{1,2},{2,3},{3,4},{4,5},{5,6},{6,7},{7,8},{8,9},{9,10},{10,1... | collective-permute-start | bytes 393224 | tf_op jit(solution)/shard_map/ppermute | solution.py:441
  5.5 7.8 %collective-permute-start.1 = (f32[8,4,1024]{2,1,0:T(4,128)}, f32[8,4,1024]{2,1,0:T(4,128)S(1)}, u32[]{:S(2)}, u32[]{:S(2)}) collective-permute-start(f32[8,4,1024]{2,1,0:T(4,128)} %get-tuple-element.16), channel_id=1, source_target_pairs={{1,0},{2,1},{3,2},{4,3},{5,4},{6,5},{7,6},{8,7},{9,8},{10,9},{11,1... | collective-permute-start | bytes 393224 | tf_op jit(solution)/shard_map/ppermute | solution.py:442
  7.3 1.4 %collective-permute-start.2 = (f32[40,128]{1,0:T(8,128)}, f32[40,128]{1,0:T(8,128)S(1)}, u32[]{:S(2)}, u32[]{:S(2)}) collective-permute-start(f32[40,128]{1,0:T(8,128)} %get-tuple-element.17), channel_id=1, source_target_pairs={{0,1},{1,0},{2,3},{3,2},{4,5},{5,4},{6,7},{7,6},{8,9},{9,8},{10,11... | collective-permute-start | bytes 61448 | tf_op jit(solution)/shard_map/ppermute | solution.py:415
  9.4 3.9 %collective-permute-start.3 = (f32[40,128]{1,0:T(8,128)S(1)}, f32[40,128]{1,0:T(8,128)S(1)}, u32[]{:S(2)}, u32[]{:S(2)}) collective-permute-start(f32[40,128]{1,0:T(8,128)S(1)} %add.31), channel_id=1, source_target_pairs={{0,2},{1,3},{2,0},{3,1},{4,6},{5,7},{6,4},{7,5},{8,10},{9,11},{10,... | collective-permute-start | bytes 61448 | tf_op jit(solution)/shard_map/ppermute | solution.py:415
  13.4 13.8 %collective-permute-start.4 = (f32[40,128]{1,0:T(8,128)S(1)}, f32[40,128]{1,0:T(8,128)S(1)}, u32[]{:S(2)}, u32[]{:S(2)}) collective-permute-start(f32[40,128]{1,0:T(8,128)S(1)} %add.32), channel_id=1, source_target_pairs={{0,4},{1,5},{2,6},{3,7},{4,0},{5,1},{6,2},{7,3},{8,12},{9,13},{10,... | collective-permute-start | bytes 61448 | tf_op jit(solution)/shard_map/ppermute | solution.py:415
  19.6 1.4 %copy-start = (f32[8,3,16,1024]{3,2,1,0:T(8,128)S(1)}, f32[8,3,16,1024]{3,2,1,0:T(8,128)}, u32[]{:S(2)}) copy-start(f32[8,3,16,1024]{3,2,1,0:T(8,128)} %tracer_ref.1) | copy-start | bytes 4718596
  21.0 1.0 %copy-start.1 = (f32[8,16,1024]{2,1,0:T(8,128)S(1)}, f32[8,16,1024]{2,1,0:T(8,128)}, u32[]{:S(2)}) copy-start(f32[8,16,1024]{2,1,0:T(8,128)} %east_ref.1) | copy-start | bytes 1572868
  22.0 1.0 %copy-start.2 = (f32[8,16,1024]{2,1,0:T(8,128)S(1)}, f32[8,16,1024]{2,1,0:T(8,128)}, u32[]{:S(2)}) copy-start(f32[8,16,1024]{2,1,0:T(8,128)} %north_ref.1) | copy-start | bytes 1572868
  23.1 0.7 copy-start.3
  27.2 12.3 %copy-start.4 = (f32[64]{0:T(128)S(1)}, f32[64]{0:T(128)}, u32[]{:S(2)}) copy-start(f32[64]{0:T(128)} %rate_ref.3) | copy-start | bytes 772
  27.2 38.7 %all-to-all-start = ((f32[8,8,3,16,128]{4,3,2,1,0:T(8,128)}), f32[8,8,3,16,128]{4,3,2,1,0:T(8,128)}, u32[]{:S(2)}, u32[]{:S(2)}) async-start(f32[8,8,3,16,128]{4,3,2,1,0:T(8,128)} %forecast.1), calls=%async_computation | async-start | bytes 3145728 | tf_op jit(solution)/shard_map/all_to_all | solution.py:449
  33.9 4.7 %collective-permute-start.5 = (f32[40,128]{1,0:T(8,128)S(1)}, f32[40,128]{1,0:T(8,128)S(1)}, u32[]{:S(2)}, u32[]{:S(2)}) collective-permute-start(f32[40,128]{1,0:T(8,128)S(1)} %add.33), channel_id=1, source_target_pairs={{0,8},{1,9},{2,10},{3,11},{4,12},{5,13},{6,14},{7,15},{8,0},{9,1},... | collective-permute-start | bytes 61448 | tf_op jit(solution)/shard_map/ppermute | solution.py:415
  38.6 7.7 %collective-permute-start.6 = (f32[40,128]{1,0:T(8,128)S(1)}, f32[40,128]{1,0:T(8,128)S(1)}, u32[]{:S(2)}, u32[]{:S(2)}) collective-permute-start(f32[40,128]{1,0:T(8,128)S(1)} %add.34), channel_id=1, source_target_pairs={{0,16},{1,17},{2,18},{3,19},{4,20},{5,21},{6,22},{7,23},{8,24},{9,... | collective-permute-start | bytes 61448 | tf_op jit(solution)/shard_map/ppermute | solution.py:415
  46.4 7.4 %collective-permute-start.7 = (f32[8,128]{1,0:T(8,128)S(1)}, f32[8,128]{1,0:T(8,128)S(1)}, u32[]{:S(2)}, u32[]{:S(2)}) collective-permute-start(f32[8,128]{1,0:T(8,128)S(1)} %fusion.1), channel_id=1, source_target_pairs={{0,32},{32,0},{64,96},{96,64},{128,160},{160,128},{192,224},{224,1... | collective-permute-start | bytes 12296 | tf_op jit(solution)/shard_map/ppermute | solution.py:415
  53.8 3.7 %collective-permute-start.8 = (f32[16,128]{1,0:T(8,128)S(1)}, f32[16,128]{1,0:T(8,128)S(1)}, u32[]{:S(2)}, u32[]{:S(2)}) collective-permute-start(f32[16,128]{1,0:T(8,128)S(1)} %pad_maximum_fusion.2), channel_id=1, source_target_pairs={{0,64},{32,96},{64,0},{96,32},{128,192},{160,224},{192,128},{224,1... | collective-permute-start | bytes 24584 | tf_op jit(solution)/shard_map/ppermute | solution.py:415
  57.5 5.2 %collective-permute-start.9 = (f32[32,128]{1,0:T(8,128)S(1)}, f32[32,128]{1,0:T(8,128)S(1)}, u32[]{:S(2)}, u32[]{:S(2)}) collective-permute-start(f32[32,128]{1,0:T(8,128)S(1)} %pad_maximum_fusion.1), channel_id=1, source_target_pairs={{0,128},{32,160},{64,192},{96,224},{128,0},{160,32},{192,64},{224,... | collective-permute-start | bytes 49160 | tf_op jit(solution)/shard_map/ppermute | solution.py:415

commit v2 on v1

v2 whole, which is shorter than its diff:
```python
import functools

import jax
import jax.numpy as jnp
from jax import lax
from jax.experimental import pallas as pl
from jax.experimental.pallas import tpu as pltpu
from jax.sharding import PartitionSpec as P

TILE_X = 32
TILE_Y = 64
LANES = 128
NONE = 999.0
LAST = 0x7FFFFFFF
PLANES = 5
STEPS = (4, 6)
VMEM_BYTES = 32 * 1024 * 1024


def lane_row(ref, *index):
    return jnp.concatenate([ref[(*index, slice(0, 1))], ref[(*index, slice(1, 2))]], axis=1)


def copies(pairs, sems):
    made = [pltpu.make_async_copy(src, dst, sems.at[i]) for i, (src, dst) in enumerate(pairs)]
    for one in made:
        one.start()
    return made


def face_flux(u_low, u_high, q_low, q_high, rate):
    face = 0.5 * (u_low + u_high)
    return (
        jnp.maximum(face, 0.0) * q_low + jnp.minimum(face, 0.0) * q_high - rate * (q_high - q_low)
    )


def prepare_kernel(
    domains, cell_hbm, tile_hbm, rate_hbm, tracer_hbm, east_hbm, north_hbm,
    inner_ref, outer_ref, meta_ref, tracer_ref, east_ref, north_ref,
    cell_ref, tile_ref, rate_ref, sems,
):
    members, levels, cols, length = tracer_ref.shape
    bands = length // LANES
    small = copies(
        [(cell_hbm, cell_ref), (tile_hbm, tile_ref), (rate_hbm, rate_ref)], sems.at[0]
    )
    loads = copies(
        [(tracer_hbm, tracer_ref), (east_hbm, east_ref), (north_hbm, north_ref)], sems.at[1]
    )
    for one in small:
        one.wait()
    domain = lax.axis_index("domain")
    me = lax.axis_index("member")
    col0 = domain * cols
    width = domains * cols
    level = lane_row(cell_ref, 0)
    x = lane_row(cell_ref, 1)
    y = lane_row(cell_ref, 2)
    ox = jnp.concatenate([tile_ref[0, 0:1], tile_ref[1, 0:1]], axis=1)
    oy = jnp.concatenate([tile_ref[0, 1:2], tile_ref[1, 1:2]], axis=1)
    lane = lax.broadcasted_iota(jnp.int32, (1, LANES), 1)
    zero = jnp.zeros((3, LANES), jnp.int32)
    meta_ref[...] = jnp.concatenate([level, x, y, ox, oy, zero], axis=0)
    near = (x >= col0) & (x < col0 + cols)
    before = jnp.where(col0 == 0, width, col0) - 1
    after = jnp.where(col0 + cols == width, 0, col0 + cols)
    near = near | (x == before) | (x == after)
    keys = jnp.where(near, (lane << 21) + (level << 19) + (x << 10) + y, LAST)
    for one in loads:
        one.wait()
    first_core = (domain & 1) == 0
    for p in range(levels + 1):
        for d in range(bands):
            at = slice(d * LANES, (d + 1) * LANES)
            plane = tracer_ref.at[:, p] if p < levels else east_ref
            low = plane[:, 0, at]
            high = plane[:, cols - 1, at]
            inner_ref[:, p * bands + d] = jnp.where(first_core, high, low)
            outer_ref[:, p * bands + d] = jnp.where(first_core, low, high)

    sub = lax.broadcasted_iota(jnp.int32, (members, LANES), 0)
    lanes = lax.broadcasted_iota(jnp.int32, (members, LANES), 1)
    rates = jnp.zeros((members, LANES), jnp.float32)
    for m in range(members):
        rates = jnp.where(sub == m, rate_ref[me * members + m], rates)

    def pick(carry):
        key, planes = carry
        following = jnp.min(jnp.where(keys > key, keys, LAST))
        k = key >> 21
        l = (key >> 19) & 3
        col = (key >> 10) & 511
        row = key & 1023
        own = (col >= col0) & (col < col0 + cols)
        here = jnp.where(own, col - col0, jnp.where(col == before, 0, cols - 1))

        def fetch(ref, lead, i, j):
            i = jnp.clip(i, 0, cols - 1)
            j = jnp.clip(j, 0, length - 1)
            first = pl.multiple_of((i >> 3) << 3, 8)
            start = pl.multiple_of((j >> 7) << 7, LANES)
            rows = jnp.zeros((members, LANES), jnp.float32)
            for m in range(members):
                tile = ref[(m, *lead, pl.ds(first, 8), pl.ds(start, LANES))]
                rows = jnp.where(sub == m, pltpu.roll(tile, (m - i) & 7, 0), rows)
            return pltpu.roll(rows, (k - (j & 127) + LANES) & 127, 1)

        q = fetch(tracer_ref, (l,), here, row)
        u = fetch(east_ref, (), here, row)
        v = fetch(north_ref, (), here, row)
        south = face_flux(
            fetch(north_ref, (), here, row - 1), v, fetch(tracer_ref, (l,), here, row - 1), q, rates
        )
        north = face_flux(
            v, fetch(north_ref, (), here, row + 1), q, fetch(tracer_ref, (l,), here, row + 1), rates
        )
        low = face_flux(
            fetch(east_ref, (), here - 1, row), u, fetch(tracer_ref, (l,), here - 1, row), q, rates
        )
        high = face_flux(
            u, fetch(east_ref, (), here + 1, row), q, fetch(tracer_ref, (l,), here + 1, row), rates
        )
        south = jnp.where(row == 0, 0.0, south)
        north = jnp.where(row == length - 1, 0.0, north)
        low = jnp.where(here == 0, 0.0, low)
        high = jnp.where(here == cols - 1, 0.0, high)
        mine = lanes == k
        ours = mine & own
        theirs = mine & jnp.logical_not(own)
        values = (
            (ours, q - (high - low) - (north - south)), (ours, q), (ours, u), (theirs, q), (theirs, u)
        )
        planes = tuple(jnp.where(at, new, old) for (at, new), old in zip(values, planes))
        return (following, planes)

    blank = jnp.zeros((members, LANES), jnp.float32)
    _, planes = lax.while_loop(
        lambda carry: carry[0] < LAST, pick, (jnp.min(keys), (blank,) * PLANES)
    )
    for i, plane in enumerate(planes):
        inner_ref[:, (levels + 1) * bands + i] = plane
    for i in range(PLANES, 8):
        inner_ref[:, (levels + 1) * bands + i] = blank


def in_hbm(*arrays):
    return [pltpu.with_memory_space_constraint(a, pltpu.HBM) for a in arrays]


def prepare(cells, tiles, rates, tracer, east, north, domains):
    members, levels, cols, length = tracer.shape
    vmem = pl.BlockSpec(memory_space=pltpu.VMEM)
    hbm = pl.BlockSpec(memory_space=pltpu.HBM)
    sent = jax.ShapeDtypeStruct(
        (members, (levels + 1) * (length // LANES) + 8, LANES), jnp.float32
    )
    return pl.pallas_call(
        functools.partial(prepare_kernel, domains),
        out_shape=[
            sent,
            sent,
            jax.ShapeDtypeStruct((8, LANES), jnp.int32),
            jax.ShapeDtypeStruct(tracer.shape, jnp.float32),
            jax.ShapeDtypeStruct(east.shape, jnp.float32),
            jax.ShapeDtypeStruct(north.shape, jnp.float32),
        ],
        in_specs=[hbm] * 6,
        out_specs=[vmem] * 6,
        scratch_shapes=[
            pltpu.VMEM(cells.shape, jnp.int32),
            pltpu.VMEM(tiles.shape, jnp.int32),
            pltpu.SMEM(rates.shape, jnp.float32),
            pltpu.SemaphoreType.DMA((2, 3)),
        ],
        compiler_params=pltpu.CompilerParams(vmem_limit_bytes=VMEM_BYTES),
        cost_estimate=pl.CostEstimate(flops=1_000_000, bytes_accessed=3_000_000, transcendentals=0),
        name="prepare",
    )(*in_hbm(cells, tiles, rates, tracer, east, north))


def face_weights(low, high, rate):
    face = 0.5 * (low + high)
    return (jnp.maximum(face, 0.0) + rate, jnp.minimum(face, 0.0) - rate)


def interior_kernel(rate_ref, tracer_ref, east_ref, north_ref, out_ref):
    members, levels, cols, length = tracer_ref.shape
    bands = out_ref.shape[0]
    me = lax.axis_index("member")
    lane = lax.broadcasted_iota(jnp.int32, (cols, LANES), 1)
    none = jnp.zeros((1, LANES), jnp.float32)

    def sides(read, d):
        here = read(d)
        left = jnp.where(lane == LANES - 1, read(d - 1), here) if d else here
        right = jnp.where(lane == 0, read(d + 1), here) if d < bands - 1 else here
        return (pltpu.roll(left, 1, 1), here, pltpu.roll(right, LANES - 1, 1))

    def member(g, carry):
        rate = rate_ref[me * members + g]
        for d in range(bands):
            at = lambda i: pl.ds(i * LANES, LANES)
            u = east_ref[g, :, at(d)]
            behind, ahead = face_weights(u[:-1], u[1:], rate)
            v_left, v, v_right = sides(lambda i: north_ref[g, :, at(i)], d)
            south_low, south_high = face_weights(v_left, v, rate)
            north_low, north_high = face_weights(v, v_right, rate)
            if d == 0:
                south_low = jnp.where(lane == 0, 0.0, south_low)
                south_high = jnp.where(lane == 0, 0.0, south_high)
            if d == bands - 1:
                north_low = jnp.where(lane == LANES - 1, 0.0, north_low)
                north_high = jnp.where(lane == LANES - 1, 0.0, north_high)
            for l in range(levels):
                q_left, q, q_right = sides(lambda i: tracer_ref[g, l, :, at(i)], d)
                flux = behind * q[:-1] + ahead * q[1:]
                flux_low = jnp.concatenate([none, flux], axis=0)
                flux_up = jnp.concatenate([flux, none], axis=0)
                south = south_low * q_left + south_high * q
                north = north_low * q + north_high * q_right
                out_ref[d, g, l] = q - (flux_up - flux_low) - (north - south)
        return carry

    lax.fori_loop(0, members, member, 0)


def interior(rates, tracer, east, north, bands):
    members, levels, cols, length = tracer.shape
    vmem = pl.BlockSpec(memory_space=pltpu.VMEM)
    return pl.pallas_call(
        interior_kernel,
        out_shape=jax.ShapeDtypeStruct((bands, members, levels, cols, LANES), jnp.float32),
        in_specs=[pl.BlockSpec(memory_space=pltpu.SMEM)] + [vmem] * 3,
        out_specs=vmem,
        compiler_params=pltpu.CompilerParams(vmem_limit_bytes=VMEM_BYTES),
        cost_estimate=pl.CostEstimate(
            flops=16_000_000, bytes_accessed=4_500_000, transcendentals=0
        ),
        name="interior",
    )(*in_hbm(rates), tracer, east, north)


def border_kernel(
    rate_ref, inner_ref, outer_ref, got_inner_ref, got_outer_ref, in_ref, out_ref
):
    bands, members, levels, cols, lanes = in_ref.shape
    me = lax.axis_index("member")
    first_core = (lax.axis_index("domain") & 1) == 0
    row = lax.broadcasted_iota(jnp.int32, (cols, lanes), 0)

    def member(g, carry):
        rate = rate_ref[me * members + g]

        def plane(p):
            at = pl.ds(p * bands, bands)
            inner, outer = inner_ref[g, at], outer_ref[g, at]
            got_inner, got_outer = got_inner_ref[g, at], got_outer_ref[g, at]
            return (
                jnp.where(first_core, got_outer, got_inner),
                jnp.where(first_core, outer, inner),
                jnp.where(first_core, inner, outer),
                jnp.where(first_core, got_inner, got_outer),
            )

        u_below, u_first, u_last, u_above = plane(levels)
        enter = face_weights(u_below, u_first, rate)
        leave = face_weights(u_last, u_above, rate)
        for l in range(levels):
            below, first, last, above = plane(l)
            low = enter[0] * below + enter[1] * first
            high = leave[0] * last + leave[1] * above
            for d in range(bands):
                change = jnp.where(
                    row == 0, low[d : d + 1], jnp.where(row == cols - 1, -high[d : d + 1], 0.0)
                )
                out_ref[d, g, l] = in_ref[d, g, l] + change
        return carry

    lax.fori_loop(0, members, member, 0)


def add_border(rates, inner, outer, got_inner, got_outer, blocks):
    vmem = pl.BlockSpec(memory_space=pltpu.VMEM)
    return pl.pallas_call(
        border_kernel,
        out_shape=jax.ShapeDtypeStruct(blocks.shape, jnp.float32),
        in_specs=[pl.BlockSpec(memory_space=pltpu.SMEM)] + [vmem] * 5,
        out_specs=vmem,
        compiler_params=pltpu.CompilerParams(vmem_limit_bytes=VMEM_BYTES),
        cost_estimate=pl.CostEstimate(flops=1_000_000, bytes_accessed=3_000_000, transcendentals=0),
        name="add_border",
    )(*in_hbm(rates), inner, outer, got_inner, got_outer, blocks)


def innovations(priors, values, errors):
    members = priors.shape[0]
    average = jnp.sum(priors, axis=0, keepdims=True) / members
    spread = priors - average
    variance = jnp.sum(spread * spread, axis=0, keepdims=True) / (members - 1)
    divisor = variance + errors
    reduction = 1.0 / (1.0 + jnp.sqrt(errors / divisor))
    factor = 1.0 / ((members - 1) * divisor)
    return (spread, values - average, reduction, factor)


def solve(priors, meta_ref, value_ref, error_ref, out_ref):
    members, total = priors.shape
    meta = meta_ref[...].astype(jnp.float32)
    across = jnp.concatenate(
        [meta, jnp.zeros((total - meta.shape[0], total), jnp.float32)], axis=0
    ).T
    level_j, x_j, y_j, ox_j, oy_j = (across[:, i : i + 1] for i in range(5))
    level_k, x_k, y_k = (meta[i : i + 1] for i in range(3))
    j_ids = lax.broadcasted_iota(jnp.int32, (total, total), 0)
    k_ids = lax.broadcasted_iota(jnp.int32, (total, total), 1)
    source = j_ids.astype(jnp.float32)
    taper_x = jnp.where(
        (x_k >= ox_j) & (x_k < ox_j + TILE_X), 1.0 - jnp.abs(x_k - x_j) / TILE_X, 0.0
    )
    taper_y = jnp.where(
        (y_k >= oy_j) & (y_k < oy_j + TILE_Y), 1.0 - jnp.abs(y_k - y_j) / TILE_Y, 0.0
    )
    weight = jnp.where(level_j == level_k, 1.0, 0.5) * taper_x * taper_y
    weight = jnp.where(j_ids < k_ids, weight, 0.0)
    pending = jnp.where(weight != 0.0, source, -1.0)
    values = lane_row(value_ref)
    errors = lane_row(error_ref)

    def following(done):
        return jnp.min(jnp.where(pending > done, pending, NONE), axis=0, keepdims=True)

    def step(carry):
        priors, nxt, left = carry
        spread, offset, reduction, factor = innovations(priors, values, errors)
        final = jnp.where(nxt == NONE, 1.0, 0.0)
        table = jnp.concatenate(
            [spread, offset, reduction, factor, final, jnp.zeros((12, total), jnp.float32)], axis=0
        )
        high = table.astype(jnp.bfloat16)
        rest = table - high.astype(jnp.float32)
        middle = rest.astype(jnp.bfloat16)
        low = (rest - middle.astype(jnp.float32)).astype(jnp.bfloat16)
        chosen = source == nxt
        pick = jnp.where(chosen, 1.0, 0.0).astype(jnp.bfloat16)
        dot = lambda part: jnp.dot(part, pick, preferred_element_type=jnp.float32)
        got = dot(high) + dot(middle) + dot(low)
        their_spread = got[:members]
        their_offset, their_reduction, their_factor, ready = (
            got[members + i : members + i + 1] for i in range(4)
        )
        rho = jnp.sum(jnp.where(chosen, weight, 0.0), axis=0, keepdims=True)
        covariance = jnp.sum(priors * their_spread, axis=0, keepdims=True)
        go = ready > 0.5
        scale = jnp.where(go, rho * covariance * their_factor, 0.0)
        priors = priors + scale * (their_offset - their_reduction * their_spread)
        done = jnp.where(go, nxt, nxt - 0.5)
        nxt = following(done)
        return (priors, nxt, jnp.min(nxt))

    nxt = following(jnp.full((1, total), -1.0, jnp.float32))
    priors, _, _ = lax.while_loop(
        lambda carry: carry[2] < NONE, step, (priors, nxt, jnp.min(nxt))
    )
    spread, offset, reduction, factor = innovations(priors, values, errors)
    out_ref[0] = spread * factor
    out_ref[1] = offset - reduction * spread


def apply_kernel(
    local_members, meta_ref, lanes_ref, near_ref, far_ref, value_ref, error_ref, in_ref,
    out_ref, table_ref, work, gain, sems
):
    members, levels, cols, rows = work.shape
    priors = jnp.concatenate([near_ref[...], far_ref[...]], axis=0)
    solve(priors, lanes_ref, value_ref, error_ref, table_ref)
    part = 8
    me = lax.axis_index("member")
    base = lax.axis_index("domain") * cols
    row0 = me * rows
    lane = lax.broadcasted_iota(jnp.int32, (1, LANES), 1)
    ox = lanes_ref[3:4]
    oy = lanes_ref[4:5]
    in_rows = (oy < row0 + rows) & (oy + TILE_Y > row0)
    half = members // local_members // 2

    def taper(position, centre, first, span):
        inside = (position >= first) & (position < first + span)
        return jnp.where(inside, 1.0 - jnp.abs(position - centre).astype(jnp.float32) / span, 0.0)

    def member_row(m):
        offset = (m // local_members) ^ me
        return ((offset >> 1) + half * (offset & 1)) * local_members + m % local_members

    keys = jnp.where(in_rows & (ox < base + cols) & (ox + TILE_X > base), lane, LAST)
    row_ids = row0 + lax.broadcasted_iota(jnp.int32, (part, rows), 1)
    near_ids = base + lax.broadcasted_iota(jnp.int32, (part, rows), 0)
    groups = cols // part
    band = lambda g: pl.ds(g * part, part)
    places = [(l, g) for l in range(levels) for g in range(groups)]

    def ready(k, slot):
        shift = (LANES - k) & 127
        for i in range(2):
            column = pltpu.roll(table_ref[i], shift, 1)[:, 0:1]
            gain[slot, i] = jnp.broadcast_to(column, (members, LANES))

    def update(k, slot, source):
        following = jnp.min(jnp.where(keys > k, keys, LAST))
        along = taper(row_ids, meta_ref[2, k], meta_ref[4, k], TILE_Y)
        weights = [
            taper(near_ids + g * part, meta_ref[1, k], meta_ref[3, k], TILE_X) * along
            for g in range(groups)
        ]
        sums = {}
        for m in range(members):
            s = gain[slot, 0, pl.ds(member_row(m), 1)]
            for l, g in places:
                term = source[m, l, band(g)] * s
                sums[l, g] = sums[l, g] + term if m else term
        scale = {}
        for l, g in places:
            vertical = jnp.where(meta_ref[0, k] == l, 1.0, 0.5)
            scale[l, g] = vertical * weights[g] * sums[l, g]
        ready(following, 1 - slot)
        for m in range(members):
            c = gain[slot, 1, pl.ds(member_row(m), 1)]
            for l, g in places:
                work[m, l, band(g)] = source[m, l, band(g)] + scale[l, g] * c
        return (following, 1 - slot)

    first = jnp.min(keys)
    store = lambda source: pltpu.make_async_copy(source, out_ref, sems.at[0])

    @pl.when(first < LAST)
    def _():
        ready(first, 0)
        second = update(first, 0, in_ref)
        lax.while_loop(lambda at: at[0] < LAST, lambda at: update(*at, work), second)
        store(work).start()

    @pl.when(first == LAST)
    def _():
        store(in_ref).start()

    store(work).wait()


def apply_updates(meta, near, far, values, errors, block, local_members):
    members, levels, cols, rows = block.shape
    vmem = pl.BlockSpec(memory_space=pltpu.VMEM)
    return pl.pallas_call(
        functools.partial(apply_kernel, local_members),
        out_shape=jax.ShapeDtypeStruct(block.shape, jnp.float32),
        in_specs=[pl.BlockSpec(memory_space=pltpu.SMEM)] + [vmem] * 6,
        out_specs=pl.BlockSpec(memory_space=pl.ANY),
        scratch_shapes=[
            pltpu.VMEM((2, members, LANES), jnp.float32),
            pltpu.VMEM(block.shape, jnp.float32),
            pltpu.VMEM((2, 2, members, LANES), jnp.float32),
            pltpu.SemaphoreType.DMA((1,)),
        ],
        compiler_params=pltpu.CompilerParams(vmem_limit_bytes=VMEM_BYTES),
        name="apply_updates",
    )(*in_hbm(meta), meta, near, far, *in_hbm(values, errors), block)


def exchange(array, axis, peers, reach):
    return lax.ppermute(array, axis, [(i, i ^ reach) for i in range(peers)])


def finish_priors(picked, meta, rates, cols):
    whole, q, u, q_far, u_far = (picked[:, i] for i in range(PLANES))
    place = meta[1:2] & (cols - 1)
    rate = rates[:, None]
    low = face_flux(u_far, u, q_far, q, rate)
    high = face_flux(u, u_far, q, q_far, rate)
    return whole + jnp.where(place == 0, low, 0.0) - jnp.where(place == cols - 1, high, 0.0)


def local(
    tracer, east_speed, north_speed, diffusivity, obs_cell, tile_offset, obs_value, obs_error
):
    members, levels, cols, length = tracer.shape
    bands = lax.axis_size("member")
    domains = lax.axis_size("domain")
    cells = obs_cell.transpose(2, 0, 1)
    tiles = tile_offset.transpose(0, 2, 1)
    rates = lax.dynamic_slice_in_dim(diffusivity, lax.axis_index("member") * members, members)
    inner, outer, meta, tracer, east, north = prepare(
        cells, tiles, diffusivity, tracer, east_speed, north_speed, domains
    )
    edges = inner.shape[1] - 8
    got_inner = exchange(inner, "domain", domains, 1)
    picked = inner[:, edges:] + got_inner[:, edges:]
    outer = jnp.concatenate([outer[:, :edges], picked], axis=1)

    def widen(picked, step):
        pairs = [((i + step if i % 2 else i - step) % domains, i) for i in range(domains)]
        return lax.ppermute(picked, "domain", pairs)

    pairs = [(i, (i + 1) % domains if i % 2 else (i - 1) % domains) for i in range(domains)]
    got_outer = lax.ppermute(outer, "domain", pairs)
    far = [widen(picked, step) for step in STEPS]
    tracer, east, north, _ = lax.optimization_barrier((tracer, east, north, outer))
    blocks = interior(diffusivity, tracer, east, north, bands)
    got_outer, far, blocks = lax.optimization_barrier((got_outer, far, blocks))
    picked = picked + got_outer[:, edges:] + sum(far)
    blocks = add_border(diffusivity, inner, outer, got_inner, got_outer, blocks)
    blocks, picked = lax.optimization_barrier((blocks, picked))
    block = lax.all_to_all(blocks, "member", split_axis=0, concat_axis=0, tiled=True)
    block = block.reshape(bands * members, levels, cols, length // bands)
    first = picked
    for step in range(8, domains, 8):
        picked = picked + widen(first, step)
    priors = finish_priors(picked, meta, rates, cols)
    near = jnp.concatenate(
        [priors] + [exchange(priors, "member", bands, reach) for reach in range(2, bands, 2)],
        axis=0,
    )
    far = exchange(near, "member", bands, 1)
    return apply_updates(meta, near, far, obs_value, obs_error, block, members)


def solution(mesh):
    placed = (
        P("member", None, "domain", None),
        P("member", "domain", None),
        P("member", "domain", None),
        P(),
        P(),
        P(),
        P(),
        P(),
    )
    return jax.shard_map(
        local,
        mesh=mesh,
        in_specs=placed,
        out_specs=P(None, None, "domain", "member"),
        check_vma=False,
    )
```

time: 72.1 us -> 56 us (0.78)
  the two profiles are of different devices: /device:TPU:74 before, /device:TPU:32 now
where the time goes in v2:
time: 56 us; the launch traced here: 55.7 us
  starting transfers between devices  29.7 us (53%)
  waiting for transfers between devices  13.7 us (24%)
  Pallas kernels  11.8 us (21%)
    ppermute x5, starting transfers between devices, widen(): return lax.ppermute(picked, 'domain', pairs)  14.8 us
    ppermute x5, waiting for transfers between devices, exchange(): return lax.ppermute(array, axis, [(i, i ^ reach) for i in range(peers)])  9.12 us
    ppermute x5, starting transfers between devices, exchange(): return lax.ppermute(array, axis, [(i, i ^ reach) for i in range(peers)])  7.48 us
    all_to_all x1, starting transfers between devices, local(): lax.all_to_all(blocks, 'member', split_axis=0, concat_axis=0, tiled=True)  6.77 us
    ppermute x5, waiting for transfers between devices, widen(): return lax.ppermute(picked, 'domain', pairs)  4.57 us
    pallas_call x1, Pallas kernels, apply_updates(): pl.pallas_call(functools.partial(apply_kernel, local_members), out_shape=...  4.32 us
    pallas_call x1, Pallas kernels, prepare(): pl.pallas_call(functools.partial(prepare_kernel, domains), out_shape=[sen...  3.02 us
    pallas_call x1, Pallas kernels, interior(): pl.pallas_call(interior_kernel, out_shape=jax.ShapeDtypeStruct((bands, me...  2.37 us
  transfers between devices with their start and end apart: 12, of which 8 were waited for; matrix products, arithmetic and copies ran while one was open for 1% of the time, Pallas kernels for 4%

profile of v2, /device:TPU:32, one launch (start us, length us, event | category | flops | bytes accessed | tf_op | source)
XLA Modules:
  0.0 55.7 jit_solution(4834632170639554083)
XLA Ops:
  0.0 3.0 %prepare.1 = (f32[8,40,128]{2,1,0:T(8,128)S(1)}, f32[8,40,128]{2,1,0:T(8,128)S(1)}, s32[8,128]{1,0:T(8,128)S(1)}, f32[8,3,16,1024]{3,2,1,0:T(8,128)S(1)}, f32[8,...) custom-call(s32[3,2,64]{2,1,0:T(2,128)} %bitcast.34, s32[2,2,64]{2,1,0:T(2,128)} %bitcast.35, f32[64]{0:T(128)} %rate_ref.3, ...), custom_call_target="tpu_custom_call" | custom-call | flops 1000000 | bytes 3000000 | tf_op jit(solution)/shard_map/prepare/pallas_call | solution.py:158
  3.0 0.0 copy-start
  3.1 0.1 collective-permute-start
  3.2 1.3 %collective-permute-done = f32[8,40,128]{2,0,1:T(8,128)S(1)} collective-permute-done((f32[8,40,128]{2,0,1:T(8,128)S(1)}, f32[8,40,128]{2,0,1:T(8,128)S(1)}, u32[]{:S(2)}, u32[]{:S(2)}) %collective-permute-start) | collective-permute-done | bytes 163872 | tf_op jit(solution)/shard_map/ppermute | solution.py:469
  4.6 0.7 %collective-permute-start.1 = (f32[8,40,128]{2,0,1:T(8,128)S(1)}, f32[8,40,128]{2,0,1:T(8,128)S(1)}, u32[]{:S(2)}, u32[]{:S(2)}) collective-permute-start(f32[8,40,128]{2,0,1:T(8,128)S(1)} %pad_maximum_fusion), channel_id=1, source_target_pairs={{0,31},{1,2},{2,1},{3,4},{4,3},{5,6},{6,5},{7,8},{8,7},{9,10},{10,... | collective-permute-start | bytes 491528 | tf_op jit(solution)/shard_map/ppermute | solution.py:503
  5.3 2.0 %collective-permute-start.2 = (f32[8,8,128]{2,0,1:T(8,128)S(1)}, f32[8,8,128]{2,0,1:T(8,128)S(1)}, u32[]{:S(2)}, u32[]{:S(2)}) collective-permute-start(f32[8,8,128]{2,0,1:T(8,128)S(1)} %slice_add_fusion), channel_id=1, source_target_pairs={{28,0},{5,1},{30,2},{7,3},{0,4},{9,5},{2,6},{11,7},{4,8},{13,9},{6... | collective-permute-start | bytes 98312 | tf_op jit(solution)/shard_map/ppermute | solution.py:500
  7.3 2.9 %collective-permute-start.3 = (f32[8,8,128]{2,0,1:T(8,128)S(1)}, f32[8,8,128]{2,0,1:T(8,128)S(1)}, u32[]{:S(2)}, u32[]{:S(2)}) collective-permute-start(f32[8,8,128]{2,0,1:T(8,128)S(1)} %slice_add_fusion), channel_id=1, source_target_pairs={{26,0},{7,1},{28,2},{9,3},{30,4},{11,5},{0,6},{13,7},{2,8},{15,9},... | collective-permute-start | bytes 98312 | tf_op jit(solution)/shard_map/ppermute | solution.py:500
  10.2 2.4 %interior.1.in_ref = f32[8,8,3,16,128]{4,3,2,1,0:T(8,128)S(1)} custom-call(f32[64]{0:T(128)} %rate_ref.3, f32[8,3,16,1024]{3,2,1,0:T(8,128)S(1)} %get-tuple-element.26.tracer_ref, f32[8,16,1024]{2,1,0:T(8,128)S(1)} %get-tuple-element.27.east_ref, f32[8,16,1024]{2,1,0:T(8,128)S(1)} %get-tuple-element.28.north_ref), custom_call_target="tpu_custom_call" | custom-call | flops 16000000 | bytes 4500000 | tf_op jit(solution)/shard_map/interior/pallas_call | solution.py:231
  12.6 0.9 %collective-permute-done.2 = f32[8,8,128]{2,0,1:T(8,128)S(1)} collective-permute-done((f32[8,8,128]{2,0,1:T(8,128)S(1)}, f32[8,8,128]{2,0,1:T(8,128)S(1)}, u32[]{:S(2)}, u32[]{:S(2)}) %collective-permute-start.2) | collective-permute-done | bytes 32800 | tf_op jit(solution)/shard_map/ppermute | solution.py:500
  13.5 1.1 %collective-permute-done.3 = f32[8,8,128]{2,0,1:T(8,128)S(1)} collective-permute-done((f32[8,8,128]{2,0,1:T(8,128)S(1)}, f32[8,8,128]{2,0,1:T(8,128)S(1)}, u32[]{:S(2)}, u32[]{:S(2)}) %collective-permute-start.3) | collective-permute-done | bytes 32800 | tf_op jit(solution)/shard_map/ppermute | solution.py:500
  14.6 0.0 collective-permute-done.1
  14.7 2.1 %add_border.1 = f32[8,8,3,16,128]{4,3,2,1,0:T(8,128)} custom-call(f32[64]{0:T(128)} %rate_ref.3, f32[8,40,128]{2,1,0:T(8,128)S(1)} %get-tuple-element.21.inner_ref, f32[8,40,128]{2,1,0:T(8,128)S(1)} %copy.12.outer_ref, f32[8,40,128]{2,1,0:T(8,128)S(1)} %copy.13.got_inner_ref, f32[8,40,128]{2,1,0:T(8,128)S(1)} %copy.14.got_outer_ref, ...), custom_call_target="tpu_custom_call" | custom-call | flops 1000000 | bytes 3000000 | tf_op jit(solution)/shard_map/add_border/pallas_call | solution.py:285
  16.8 0.0 copy-start.1
  16.8 6.8 %all-to-all-start = ((f32[8,8,3,16,128]{4,3,2,1,0:T(8,128)}), f32[8,8,3,16,128]{4,3,2,1,0:T(8,128)S(1)}, u32[]{:S(2)}, u32[]{:S(2)}) async-start(f32[8,8,3,16,128]{4,3,2,1,0:T(8,128)} %add_border.1), calls=%async_computation | async-start | bytes 3145728 | tf_op jit(solution)/shard_map/all_to_all | solution.py:511
  23.5 2.6 %collective-permute-start.4 = (f32[8,8,128]{2,0,1:T(8,128)S(1)}, f32[8,8,128]{2,0,1:T(8,128)S(1)}, u32[]{:S(2)}, u32[]{:S(2)}) collective-permute-start(f32[8,8,128]{2,0,1:T(8,128)S(1)} %add_add_fusion.1), channel_id=1, source_target_pairs={{24,0},{9,1},{26,2},{11,3},{28,4},{13,5},{30,6},{15,7},{0,8},{17,9... | collective-permute-start | bytes 98312 | tf_op jit(solution)/shard_map/ppermute | solution.py:500
  26.1 5.2 %collective-permute-start.5 = (f32[8,8,128]{2,0,1:T(8,128)S(1)}, f32[8,8,128]{2,0,1:T(8,128)S(1)}, u32[]{:S(2)}, u32[]{:S(2)}) collective-permute-start(f32[8,8,128]{2,0,1:T(8,128)S(1)} %add_add_fusion.1), channel_id=1, source_target_pairs={{16,0},{17,1},{18,2},{19,3},{20,4},{21,5},{22,6},{23,7},{24,8},{25... | collective-permute-start | bytes 98312 | tf_op jit(solution)/shard_map/ppermute | solution.py:500
  31.3 2.2 %collective-permute-start.6 = (f32[8,8,128]{2,0,1:T(8,128)S(1)}, f32[8,8,128]{2,0,1:T(8,128)S(1)}, u32[]{:S(2)}, u32[]{:S(2)}) collective-permute-start(f32[8,8,128]{2,0,1:T(8,128)S(1)} %add_add_fusion.1), channel_id=1, source_target_pairs={{8,0},{25,1},{10,2},{27,3},{12,4},{29,5},{14,6},{31,7},{16,8},{1,9... | collective-permute-start | bytes 98312 | tf_op jit(solution)/shard_map/ppermute | solution.py:500
  33.5 0.0 copy-done
  33.5 0.0 copy-done.1
  33.5 0.1 dynamic_slice.3
  33.6 0.0 collective-permute-done.4
  33.6 0.4 collective-permute-done.5
  33.9 2.2 %collective-permute-done.6 = f32[8,8,128]{2,0,1:T(8,128)S(1)} collective-permute-done((f32[8,8,128]{2,0,1:T(8,128)S(1)}, f32[8,8,128]{2,0,1:T(8,128)S(1)}, u32[]{:S(2)}, u32[]{:S(2)}) %collective-permute-start.6) | collective-permute-done | bytes 32800 | tf_op jit(solution)/shard_map/ppermute | solution.py:500
  36.1 0.1 fusion.2
  36.2 2.1 %collective-permute-start.7 = (f32[8,128]{1,0:T(8,128)S(1)}, f32[8,128]{1,0:T(8,128)S(1)}, u32[]{:S(2)}, u32[]{:S(2)}) collective-permute-start(f32[8,128]{1,0:T(8,128)S(1)} %fusion.2), channel_id=1, source_target_pairs={{0,64},{32,96},{64,0},{96,32},{128,192},{160,224},{192,128},{224,1... | collective-permute-start | bytes 12296 | tf_op jit(solution)/shard_map/ppermute | solution.py:469
  38.2 2.7 %collective-permute-start.8 = (f32[8,128]{1,0:T(8,128)S(1)}, f32[8,128]{1,0:T(8,128)S(1)}, u32[]{:S(2)}, u32[]{:S(2)}) collective-permute-start(f32[8,128]{1,0:T(8,128)S(1)} %fusion.2), channel_id=1, source_target_pairs={{0,128},{32,160},{64,192},{96,224},{128,0},{160,32},{192,64},{224,... | collective-permute-start | bytes 12296 | tf_op jit(solution)/shard_map/ppermute | solution.py:469
  40.9 0.1 collective-permute-start.9
  41.0 2.8 %collective-permute-done.7 = f32[8,128]{1,0:T(8,128)S(1)} collective-permute-done((f32[8,128]{1,0:T(8,128)S(1)}, f32[8,128]{1,0:T(8,128)S(1)}, u32[]{:S(2)}, u32[]{:S(2)}) %collective-permute-start.7) | collective-permute-done | bytes 4128 | tf_op jit(solution)/shard_map/ppermute | solution.py:469
  43.8 0.0 collective-permute-done.8
  43.8 2.4 %collective-permute-done.9 = f32[8,128]{1,0:T(8,128)S(1)} collective-permute-done((f32[8,128]{1,0:T(8,128)S(1)}, f32[8,128]{1,0:T(8,128)S(1)}, u32[]{:S(2)}, u32[]{:S(2)}) %collective-permute-start.9) | collective-permute-done | bytes 4128 | tf_op jit(solution)/shard_map/ppermute | solution.py:469
  46.1 2.6 %collective-permute-start.10 = (f32[32,128]{1,0:T(8,128)S(1)}, f32[32,128]{1,0:T(8,128)S(1)}, u32[]{:S(2)}, u32[]{:S(2)}) collective-permute-start(f32[32,128]{1,0:T(8,128)S(1)} %pad_maximum_fusion.1.near_ref), channel_id=1, source_target_pairs={{0,32},{32,0},{64,96},{96,64},{128,160},{160,128},{192,224},{224,1... | collective-permute-start | bytes 49160 | tf_op jit(solution)/shard_map/ppermute | solution.py:469
  48.7 2.7 %collective-permute-done.10.far_ref = f32[32,128]{1,0:T(8,128)S(1)} collective-permute-done((f32[32,128]{1,0:T(8,128)S(1)}, f32[32,128]{1,0:T(8,128)S(1)}, u32[]{:S(2)}, u32[]{:S(2)}) %collective-permute-start.10) | collective-permute-done | bytes 16416 | tf_op jit(solution)/shard_map/ppermute | solution.py:469
  51.4 0.0 all-to-all-done
  51.4 4.3 %apply_updates.1 = f32[64,3,16,128]{3,2,1,0:T(8,128)} custom-call(s32[8,128]{1,0:T(8,128)} %copy-done, s32[8,128]{1,0:T(8,128)} %copy-done, f32[32,128]{1,0:T(8,128)S(1)} %pad_maximum_fusion.1.near_ref, f32[32,128]{1,0:T(8,128)S(1)} %collective-permute-done.10.far_ref, f32[2,64]{1,0:T(2,128)} %value_ref.1, f32[2,64]{1,0:T(2,128)} %error_ref.1, ...), custom_call_target="tpu_custom_call" | custom-call | tf_op jit(solution)/shard_map/apply_updates/pallas_call | solution.py:452
  (12 shorter events, 0.2 us)
Async XLA Ops:
  3.0 30.4 %copy-start = (s32[8,128]{1,0:T(8,128)}, s32[8,128]{1,0:T(8,128)S(1)}, u32[]{:S(2)}) copy-start(s32[8,128]{1,0:T(8,128)S(1)} %get-tuple-element.20.meta_ref.lanes_ref) | copy-start | bytes 12292
  3.1 1.5 %collective-permute-start = (f32[8,40,128]{2,0,1:T(8,128)S(1)}, f32[8,40,128]{2,0,1:T(8,128)S(1)}, u32[]{:S(2)}, u32[]{:S(2)}) collective-permute-start(f32[8,40,128]{2,0,1:T(8,128)S(1)} %copy.10), channel_id=1, source_target_pairs={{0,1},{1,0},{2,3},{3,2},{4,5},{5,4},{6,7},{7,6},{8,9},{9,8},{10,11... | collective-permute-start | bytes 491528 | tf_op jit(solution)/shard_map/ppermute | solution.py:469
  4.6 10.0 %collective-permute-start.1 = (f32[8,40,128]{2,0,1:T(8,128)S(1)}, f32[8,40,128]{2,0,1:T(8,128)S(1)}, u32[]{:S(2)}, u32[]{:S(2)}) collective-permute-start(f32[8,40,128]{2,0,1:T(8,128)S(1)} %pad_maximum_fusion), channel_id=1, source_target_pairs={{0,31},{1,2},{2,1},{3,4},{4,3},{5,6},{6,5},{7,8},{8,7},{9,10},{10,... | collective-permute-start | bytes 491528 | tf_op jit(solution)/shard_map/ppermute | solution.py:503
  5.3 8.2 %collective-permute-start.2 = (f32[8,8,128]{2,0,1:T(8,128)S(1)}, f32[8,8,128]{2,0,1:T(8,128)S(1)}, u32[]{:S(2)}, u32[]{:S(2)}) collective-permute-start(f32[8,8,128]{2,0,1:T(8,128)S(1)} %slice_add_fusion), channel_id=1, source_target_pairs={{28,0},{5,1},{30,2},{7,3},{0,4},{9,5},{2,6},{11,7},{4,8},{13,9},{6... | collective-permute-start | bytes 98312 | tf_op jit(solution)/shard_map/ppermute | solution.py:500
  7.3 7.3 %collective-permute-start.3 = (f32[8,8,128]{2,0,1:T(8,128)S(1)}, f32[8,8,128]{2,0,1:T(8,128)S(1)}, u32[]{:S(2)}, u32[]{:S(2)}) collective-permute-start(f32[8,8,128]{2,0,1:T(8,128)S(1)} %slice_add_fusion), channel_id=1, source_target_pairs={{26,0},{7,1},{28,2},{9,3},{30,4},{11,5},{0,6},{13,7},{2,8},{15,9},... | collective-permute-start | bytes 98312 | tf_op jit(solution)/shard_map/ppermute | solution.py:500
  16.8 16.7 %copy-start.1 = (f32[64]{0:T(128)S(1)}, f32[64]{0:T(128)}, u32[]{:S(2)}) copy-start(f32[64]{0:T(128)} %rate_ref.3) | copy-start | bytes 772
  16.8 34.6 %all-to-all-start = ((f32[8,8,3,16,128]{4,3,2,1,0:T(8,128)}), f32[8,8,3,16,128]{4,3,2,1,0:T(8,128)S(1)}, u32[]{:S(2)}, u32[]{:S(2)}) async-start(f32[8,8,3,16,128]{4,3,2,1,0:T(8,128)} %add_border.1), calls=%async_computation | async-start | bytes 3145728 | tf_op jit(solution)/shard_map/all_to_all | solution.py:511
  23.5 10.0 %collective-permute-start.4 = (f32[8,8,128]{2,0,1:T(8,128)S(1)}, f32[8,8,128]{2,0,1:T(8,128)S(1)}, u32[]{:S(2)}, u32[]{:S(2)}) collective-permute-start(f32[8,8,128]{2,0,1:T(8,128)S(1)} %add_add_fusion.1), channel_id=1, source_target_pairs={{24,0},{9,1},{26,2},{11,3},{28,4},{13,5},{30,6},{15,7},{0,8},{17,9... | collective-permute-start | bytes 98312 | tf_op jit(solution)/shard_map/ppermute | solution.py:500
  26.1 7.8 %collective-permute-start.5 = (f32[8,8,128]{2,0,1:T(8,128)S(1)}, f32[8,8,128]{2,0,1:T(8,128)S(1)}, u32[]{:S(2)}, u32[]{:S(2)}) collective-permute-start(f32[8,8,128]{2,0,1:T(8,128)S(1)} %add_add_fusion.1), channel_id=1, source_target_pairs={{16,0},{17,1},{18,2},{19,3},{20,4},{21,5},{22,6},{23,7},{24,8},{25... | collective-permute-start | bytes 98312 | tf_op jit(solution)/shard_map/ppermute | solution.py:500
  31.3 4.8 %collective-permute-start.6 = (f32[8,8,128]{2,0,1:T(8,128)S(1)}, f32[8,8,128]{2,0,1:T(8,128)S(1)}, u32[]{:S(2)}, u32[]{:S(2)}) collective-permute-start(f32[8,8,128]{2,0,1:T(8,128)S(1)} %add_add_fusion.1), channel_id=1, source_target_pairs={{8,0},{25,1},{10,2},{27,3},{12,4},{29,5},{14,6},{31,7},{16,8},{1,9... | collective-permute-start | bytes 98312 | tf_op jit(solution)/shard_map/ppermute | solution.py:500
  36.2 7.6 %collective-permute-start.7 = (f32[8,128]{1,0:T(8,128)S(1)}, f32[8,128]{1,0:T(8,128)S(1)}, u32[]{:S(2)}, u32[]{:S(2)}) collective-permute-start(f32[8,128]{1,0:T(8,128)S(1)} %fusion.2), channel_id=1, source_target_pairs={{0,64},{32,96},{64,0},{96,32},{128,192},{160,224},{192,128},{224,1... | collective-permute-start | bytes 12296 | tf_op jit(solution)/shard_map/ppermute | solution.py:469
  38.2 5.5 %collective-permute-start.8 = (f32[8,128]{1,0:T(8,128)S(1)}, f32[8,128]{1,0:T(8,128)S(1)}, u32[]{:S(2)}, u32[]{:S(2)}) collective-permute-start(f32[8,128]{1,0:T(8,128)S(1)} %fusion.2), channel_id=1, source_target_pairs={{0,128},{32,160},{64,192},{96,224},{128,0},{160,32},{192,64},{224,... | collective-permute-start | bytes 12296 | tf_op jit(solution)/shard_map/ppermute | solution.py:469
  40.9 5.2 %collective-permute-start.9 = (f32[8,128]{1,0:T(8,128)S(1)}, f32[8,128]{1,0:T(8,128)S(1)}, u32[]{:S(2)}, u32[]{:S(2)}) collective-permute-start(f32[8,128]{1,0:T(8,128)S(1)} %fusion.2), channel_id=1, source_target_pairs={{0,192},{32,224},{64,128},{96,160},{128,64},{160,96},{192,0},{224,... | collective-permute-start | bytes 12296 | tf_op jit(solution)/shard_map/ppermute | solution.py:469
  46.1 5.2 %collective-permute-start.10 = (f32[32,128]{1,0:T(8,128)S(1)}, f32[32,128]{1,0:T(8,128)S(1)}, u32[]{:S(2)}, u32[]{:S(2)}) collective-permute-start(f32[32,128]{1,0:T(8,128)S(1)} %pad_maximum_fusion.1.near_ref), channel_id=1, source_target_pairs={{0,32},{32,0},{64,96},{96,64},{128,160},{160,128},{192,224},{224,1... | collective-permute-start | bytes 49160 | tf_op jit(solution)/shard_map/ppermute | solution.py:469
